TPU v7x, 128 devices: a whole 4x4x4 slice. The times are simulated.
128 devices in a mesh: front: 2 (over core), row: 4 (over y), col: 16 (over x, z).
Axes of the slice: x: 4, y: 4, z: 4, core: 2. Of those that a mesh axis runs over, the one named last changes fastest.
Arguments:
- child_fronts: float32 [4, 6144, 6144], P('front', 'row', 'col'), as said below
- parent_front: float32 [12288, 12288], P('row', ('front', 'col')), as said below
- child_inverses: float32 [4, 2, 128, 128], P('front'), as said below
- parent_inverses: float32 [5, 128, 128], replicated, as said below
- block_map: int32 [4, 48], P('front'), may hold values from -1 to 95, as said below
Outputs:
- parent_factor: float32 [12288, 12288], P('row', ('front', 'col'))
Inputs may be any that keep to these rules, and one draw needn't show every extreme that they name: `child_fronts`: each child front is symmetric in logical order. `parent_front`: the parent front is symmetric in logical order. `child_inverses`: every block is symmetric. `parent_inverses`: every block is symmetric. `block_map`: entry [c, j] is -1 exactly for the pivot blocks j < 2; otherwise it is the parent block that child block j of child c is added into. Child c belongs to front group g = c // 2, and its blocks land on parent blocks p with p % 32 between g * 16 and g * 16 + 15. Distinct blocks of one child land on distinct parent blocks. For each front group there is one offset per child of the group and per t = j // 16 such that block j lands on a parent block congruent to j plus that offset modulo 16. Among the contribution blocks of the 2 children of a group with one value of j % 16, at most 1 land on parent blocks with one value of p % 16; among those with one value of j % 4, at most 8 land on parent blocks with one value of p % 4. Both bounds are reached in every draw.
All inputs are finite; a program needn't handle non-finite values.
Results may differ from a plain program's by a relative error of at most 0.0003.
Values sent between devices are 32-bit elements; how exact they have to be, the bound alone decides.
A program may use at most 256 MiB of HBM per device.

v0:
```python
import jax
import jax.numpy as jnp
from jax import lax
from jax.sharding import PartitionSpec as P

HIGHEST = lax.Precision.HIGHEST


def from_root(value, axis, source):
    kept = jnp.where(lax.axis_index(axis) == source, value, 0).astype(value.dtype)
    return lax.psum(kept, axis)


def product(first, second):
    return jnp.dot(first, second, precision=HIGHEST, preferred_element_type=jnp.float32)


def renew(matrix, column, across, inverse, row_blocks, col_blocks, pivot_step):
    block_size = inverse.shape[0]
    scaled_cols = product(column, inverse)
    scaled_rows = product(inverse, across)
    later_rows = (row_blocks > pivot_step)[:, None]
    later_cols = (col_blocks > pivot_step)[None, :]
    pivot_rows = (row_blocks == pivot_step)[:, None]
    pivot_cols = (col_blocks == pivot_step)[None, :]
    result = jnp.where(later_rows & later_cols, matrix - product(scaled_cols, across), matrix)
    result = jnp.where(
        later_rows & pivot_cols, jnp.tile(scaled_cols, (1, matrix.shape[1] // block_size)), result
    )
    return jnp.where(
        pivot_rows & later_cols, jnp.tile(scaled_rows, (matrix.shape[0] // block_size, 1)), result
    )


def slot_table(targets, owners, capacity):
    flattened = targets.reshape(-1)
    usable = flattened >= 0
    owner_of = jnp.where(usable, flattened % owners, -1)
    positions = jnp.arange(flattened.shape[0])
    earlier = (
        (owner_of[:, None] == owner_of[None, :])
        & usable[None, :]
        & (positions[None, :] < positions[:, None])
    )
    ranking = jnp.sum(earlier.astype(jnp.int32), axis=1)
    owner_ids = jnp.arange(owners)[:, None, None]
    slot_ids = jnp.arange(capacity)[None, :, None]
    return (
        (owner_of[None, None, :] == owner_ids)
        & (ranking[None, None, :] == slot_ids)
        & usable[None, None, :]
    )


def slot_tags(slot_hits, codes):
    return jnp.sum(jnp.where(slot_hits, codes[None, None, :] + 1, 0), axis=2) - 1


def body(child_fronts, parent_front, child_inverses, parent_inverses, block_map):
    block_size = child_inverses.shape[-1]
    row_count = lax.axis_size("row")
    col_count = lax.axis_size("col")
    grid_cols = lax.axis_size(("front", "col"))
    row_index = lax.axis_index("row")
    col_index = lax.axis_index("col")
    grid_index = lax.axis_index(("front", "col"))
    kid_count, local_rows, local_cols = child_fronts.shape
    child_row_blocks = jnp.arange(local_rows) // block_size * row_count + row_index
    child_col_blocks = jnp.arange(local_cols) // block_size * col_count + col_index
    fronts = child_fronts
    for pivot_step in range(child_inverses.shape[1]):
        col_start = pivot_step // col_count * block_size
        row_start = pivot_step // row_count * block_size
        column = from_root(
            fronts[:, :, col_start : col_start + block_size], "col", pivot_step % col_count
        )
        across = from_root(
            fronts[:, row_start : row_start + block_size, :], "row", pivot_step % row_count
        )
        fronts = jax.vmap(
            lambda matrix, panel, strip, inverse: renew(
                matrix, panel, strip, inverse, child_row_blocks, child_col_blocks, pivot_step
            )
        )(fronts, column, across, child_inverses[:, pivot_step])
    col_slots = local_cols // block_size
    parent_col_slots = parent_front.shape[1] // block_size
    map_view = block_map.reshape(kid_count, col_slots, col_count)
    col_targets = lax.dynamic_index_in_dim(map_view, col_index, 2, keepdims=False)
    col_cap = (kid_count * col_slots + col_count - 1) // col_count
    slot_hits = slot_table(col_targets, col_count, col_cap)
    col_codes = jnp.where(
        col_targets >= 0,
        jnp.arange(kid_count)[:, None] * parent_col_slots + col_targets // grid_cols,
        -1,
    ).reshape(-1)
    col_tags = slot_tags(slot_hits, col_codes)
    selector = slot_hits.reshape(col_count, col_cap, kid_count, col_slots).astype(jnp.float32)
    outgoing = jnp.einsum(
        "dsct,crtb->dsrb",
        selector,
        fronts.reshape(kid_count, local_rows, col_slots, block_size),
        precision=HIGHEST,
    )
    incoming, incoming_tags = (
        lax.all_to_all(outgoing, "col", split_axis=0, concat_axis=0, tiled=True),
        lax.all_to_all(col_tags, "col", split_axis=0, concat_axis=0, tiled=True),
    )
    wanted = (
        jnp.arange(kid_count)[:, None] * parent_col_slots + jnp.arange(parent_col_slots)[None, :]
    )
    placing = (incoming_tags[None, None, :, :] == wanted[:, :, None, None]).astype(jnp.float32)
    landed = jnp.einsum("cusk,skrb->crub", placing, incoming, precision=HIGHEST).reshape(
        kid_count, local_rows, parent_col_slots * block_size
    )
    row_slots = local_rows // block_size
    row_view = block_map.reshape(kid_count, row_slots, row_count)
    row_targets = lax.dynamic_index_in_dim(row_view, row_index, 2, keepdims=False)
    row_cap = col_count // row_count * ((kid_count * col_slots + row_count - 1) // row_count)
    row_hits = slot_table(row_targets, row_count, row_cap)
    row_codes = jnp.where(row_targets >= 0, row_targets // row_count, -1).reshape(-1)
    row_tags = slot_tags(row_hits, row_codes)
    row_selector = row_hits.reshape(row_count, row_cap, kid_count, row_slots).astype(jnp.float32)
    strips = landed.reshape(kid_count, row_slots, block_size, landed.shape[2])
    row_outgoing = jnp.einsum("dscl,clbk->dsbk", row_selector, strips, precision=HIGHEST)
    row_incoming, row_incoming_tags = (
        lax.all_to_all(row_outgoing, "row", split_axis=0, concat_axis=0, tiled=True),
        lax.all_to_all(row_tags, "row", split_axis=0, concat_axis=0, tiled=True),
    )
    parent_row_slots = parent_front.shape[0] // block_size
    row_placing = (
        row_incoming_tags[None, :, :] == jnp.arange(parent_row_slots)[:, None, None]
    ).astype(jnp.float32)
    assembled = jnp.einsum("psk,skbc->pbc", row_placing, row_incoming, precision=HIGHEST).reshape(
        parent_front.shape
    )
    matrix = parent_front + assembled
    parent_row_blocks = jnp.arange(parent_front.shape[0]) // block_size * row_count + row_index
    parent_col_blocks = jnp.arange(parent_front.shape[1]) // block_size * grid_cols + grid_index
    steps_total = parent_inverses.shape[0]
    for pivot_step in range(steps_total):
        col_start = pivot_step // grid_cols * block_size
        row_start = pivot_step // row_count * block_size
        panels_column = from_root(
            matrix[:, col_start : col_start + block_size], ("front", "col"), pivot_step % grid_cols
        )
        mirror = from_root(panels_column, "row", grid_index % row_count)
        fold_count = grid_cols // row_count
        shaped = mirror.reshape(
            mirror.shape[0] // (block_size * fold_count), fold_count, block_size, block_size
        )
        picked = lax.dynamic_index_in_dim(shaped, grid_index // row_count, 1, keepdims=False)
        panels_across = picked.reshape(-1, block_size).T
        column = panels_column
        across = panels_across
        matrix = renew(
            matrix,
            column,
            across,
            parent_inverses[pivot_step],
            parent_row_blocks,
            parent_col_blocks,
            pivot_step,
        )
    return matrix


def solution(mesh):
    placed = (
        P("front", "row", "col"),
        P("row", ("front", "col")),
        P("front", None, None, None),
        P(),
        P("front", None),
    )
    return jax.shard_map(
        body, mesh=mesh, in_specs=placed, out_specs=P("row", ("front", "col")), check_vma=False
    )
```

profile of v0, /device:TPU:1, one launch (start us, length us, event | category | flops | bytes accessed | tf_op | source)
XLA Modules:
  0.0 1567.1 jit_solution(16156913744828403604)
XLA Ops:
  20.3 37.5 %all-reduce.15.cloned.1.call-done = f32[2,128,384]{1,2,0:T(8,128)} async-done(((f32[2,128,384]{1,2,0:T(8,128)}), f32[2,128,384]{1,2,0:T(8,128)}) %all-reduce.15.cloned.1.call-update) | async-done | bytes 393232 | tf_op jit(solution)/shard_map/psum | solution.py:11
  68.2 83.2 %all-reduce.17.cloned.1.call-done = f32[2,1536,128]{1,2,0:T(8,128)} async-done(((f32[2,1536,128]{1,2,0:T(8,128)}), f32[2,1536,128]{1,2,0:T(8,128)}) %all-reduce.17.cloned.1.call-update) | async-done | bytes 1572880 | tf_op jit(solution)/shard_map/psum | solution.py:11
  156.5 8.3 fusion.7
  178.6 30.0 %all-reduce.19.cloned.1.call-done = f32[2,128,384]{1,2,0:T(8,128)} async-done(((f32[2,128,384]{1,2,0:T(8,128)}), f32[2,128,384]{1,2,0:T(8,128)}) %all-reduce.19.cloned.1.call-update) | async-done | bytes 393232 | tf_op jit(solution)/shard_map/psum | solution.py:11
  219.1 82.7 %all-reduce.21.cloned.1.call-done = f32[2,1536,128]{1,2,0:T(8,128)} async-done(((f32[2,1536,128]{1,2,0:T(8,128)}), f32[2,1536,128]{1,2,0:T(8,128)}) %all-reduce.21.cloned.1.call-update) | async-done | bytes 1572880 | tf_op jit(solution)/shard_map/psum | solution.py:11
  306.8 9.6 fusion.9
  323.5 12.2 convolution_bitcast_fusion
  335.7 13.1 copy.148
  355.9 213.1 %all-to-all-done.1 = f32[16,1,1536,128]{3,2,1,0:T(8,128)} async-done(((f32[16,1,1536,128]{3,2,1,0:T(8,128)}), f32[16,1,1536,128]{3,2,1,0:T(8,128)}, u32[]{:S(2)}, u32[]{:S(2)}) %all-to-all-start.1) | async-done | bytes 12582944 | tf_op jit(solution)/shard_map/all_to_all | solution.py:105
  573.0 21.3 %fusion.23 = f32[2,1536,3,128]{3,2,0,1:T(4,128)} fusion(f32[16,1,1536,128]{3,2,1,0:T(8,128)} %all-to-all-done.1, s32[2,3]{1,0:T(2,128)S(1)} %iota_add_fusion, s32[16]{0:T(128)S(1)} %reduce.4), kind=kOutput, calls=%fused_computation.30 | convolution fusion | flops 226492512 | bytes 17301592 | tf_op jit(solution)/shard_map/cusk,skrb->crub/dot_general | solution.py:112
  594.3 9.4 reshape.838
  603.6 11.0 fusion.20
  620.1 66.3 %all-to-all-done.3 = f32[4,8,128,384]{3,1,2,0:T(8,128)} async-done(((f32[4,8,128,384]{3,1,2,0:T(8,128)}), f32[4,8,128,384]{3,1,2,0:T(8,128)}, u32[]{:S(2)}, u32[]{:S(2)}) %all-to-all-start.3) | async-done | bytes 6291488 | tf_op jit(solution)/shard_map/all_to_all | solution.py:126
  696.4 114.3 %all-reduce.23.cloned.1.call-done = f32[3072,128]{1,0:T(8,128)} async-done(((f32[3072,128]{1,0:T(8,128)}), f32[3072,128]{1,0:T(8,128)}) %all-reduce.23.cloned.1.call-update) | async-done | bytes 1572880 | tf_op jit(solution)/shard_map/psum | solution.py:11
  826.0 37.3 %all-reduce.25.cloned.1.call-done = f32[3,8,128,128]{3,2,1,0:T(8,128)} async-done(((f32[3,8,128,128]{3,2,1,0:T(8,128)}), f32[3,8,128,128]{3,2,1,0:T(8,128)}) %all-reduce.25.cloned.1.call-update) | async-done | bytes 1572880 | tf_op jit(solution)/shard_map/psum | solution.py:11
  875.8 106.6 %all-reduce.27.cloned.1.call-done = f32[3072,128]{1,0:T(8,128)} async-done(((f32[3072,128]{1,0:T(8,128)}), f32[3072,128]{1,0:T(8,128)}) %all-reduce.27.cloned.1.call-update) | async-done | bytes 1572880 | tf_op jit(solution)/shard_map/psum | solution.py:11
  997.3 37.5 %all-reduce.29.cloned.1.call-done = f32[3,8,128,128]{3,2,1,0:T(8,128)} async-done(((f32[3,8,128,128]{3,2,1,0:T(8,128)}), f32[3,8,128,128]{3,2,1,0:T(8,128)}) %all-reduce.29.cloned.1.call-update) | async-done | bytes 1572880 | tf_op jit(solution)/shard_map/psum | solution.py:11
  1047.3 106.6 %all-reduce.31.cloned.1.call-done = f32[3072,128]{1,0:T(8,128)} async-done(((f32[3072,128]{1,0:T(8,128)}), f32[3072,128]{1,0:T(8,128)}) %all-reduce.31.cloned.1.call-update) | async-done | bytes 1572880 | tf_op jit(solution)/shard_map/psum | solution.py:11
  1169.1 37.3 %all-reduce.33.cloned.1.call-done = f32[3,8,128,128]{3,2,1,0:T(8,128)} async-done(((f32[3,8,128,128]{3,2,1,0:T(8,128)}), f32[3,8,128,128]{3,2,1,0:T(8,128)}) %all-reduce.33.cloned.1.call-update) | async-done | bytes 1572880 | tf_op jit(solution)/shard_map/psum | solution.py:11
  1218.8 106.6 %all-reduce.35.cloned.1.call-done = f32[3072,128]{1,0:T(8,128)} async-done(((f32[3072,128]{1,0:T(8,128)}), f32[3072,128]{1,0:T(8,128)}) %all-reduce.35.cloned.1.call-update) | async-done | bytes 1572880 | tf_op jit(solution)/shard_map/psum | solution.py:11
  1340.4 37.5 %all-reduce.37.cloned.1.call-done = f32[3,8,128,128]{3,2,1,0:T(8,128)} async-done(((f32[3,8,128,128]{3,2,1,0:T(8,128)}), f32[3,8,128,128]{3,2,1,0:T(8,128)}) %all-reduce.37.cloned.1.call-update) | async-done | bytes 1572880 | tf_op jit(solution)/shard_map/psum | solution.py:11
  1390.4 106.6 %all-reduce.39.cloned.1.call-done = f32[3072,128]{1,0:T(8,128)} async-done(((f32[3072,128]{1,0:T(8,128)}), f32[3072,128]{1,0:T(8,128)}) %all-reduce.39.cloned.1.call-update) | async-done | bytes 1572880 | tf_op jit(solution)/shard_map/psum | solution.py:11
  1512.3 37.2 %all-reduce.41.cloned.1.call-done = f32[3,8,128,128]{3,2,1,0:T(8,128)} async-done(((f32[3,8,128,128]{3,2,1,0:T(8,128)}), f32[3,8,128,128]{3,2,1,0:T(8,128)}) %all-reduce.41.cloned.1.call-update) | async-done | bytes 1572880 | tf_op jit(solution)/shard_map/psum | solution.py:11
  1550.9 9.1 fusion.19
  (199 shorter events, 218.1 us)
Async XLA Ops:
  6.5 51.3 %all-reduce.15.cloned.1.call-start = ((), (), s32[]{:S(2)}) async-start(), calls=%async_computation.4 | async-start | bytes 786432 | tf_op jit(solution)/shard_map/psum | solution.py:11
  14.4 137.0 %all-reduce.17.cloned.1.call-start = ((), (), s32[]{:S(2)}) async-start(), calls=%async_computation.5 | async-start | bytes 3145728 | tf_op jit(solution)/shard_map/psum | solution.py:11
  17.2 40.7 %copy-start.14 = (f32[2,2,128,128]{3,2,1,0:T(8,128)S(1)}, f32[2,2,128,128]{3,2,1,0:T(8,128)}, u32[]{:S(2)}) copy-start(f32[2,2,128,128]{3,2,1,0:T(8,128)} %param.7) | copy-start | bytes 786436
  17.2 191.5 %all-reduce.19.cloned.1.call-start = ((), (), s32[]{:S(2)}) async-start(), calls=%async_computation.6 | async-start | bytes 786432 | tf_op jit(solution)/shard_map/psum | solution.py:11
  17.3 40.5 %copy-start.19 = (s32[2]{0:T(128)}, s32[2]{0:T(128)S(1)}, u32[]{:S(2)}) copy-start(s32[2]{0:T(128)S(1)} %iota_multiply_fusion) | copy-start | bytes 28
  18.6 152.0 %copy-start.18 = (pred[6]{0:T(512)(128)(4,1)}, pred[6]{0:T(512)(128)(4,1)S(1)}, u32[]{:S(2)}) copy-start(pred[6]{0:T(512)(128)(4,1)S(1)} %broadcast_compare_fusion.15) | copy-start | bytes 22
  167.8 134.1 %all-reduce.21.cloned.1.call-start = ((), (), s32[]{:S(2)}) async-start(), calls=%async_computation.7 | async-start | bytes 3145728 | tf_op jit(solution)/shard_map/psum | solution.py:11
  170.5 38.2 %copy-start.15 = (f32[2,2,128,128]{3,2,1,0:T(8,128)S(1)}, f32[2,2,128,128]{3,2,1,0:T(8,128)}, u32[]{:S(2)}) copy-start(f32[2,2,128,128]{3,2,1,0:T(8,128)} %param.7) | copy-start | bytes 786436
  171.3 177.5 %all-to-all-start.2 = ((s32[16,1,1]{2,1,0:T(1,128)}), s32[16,1,1]{2,1,0:T(1,128)S(1)}, u32[]{:S(2)}, u32[]{:S(2)}) async-start(s32[16,1,1]{2,1,0:T(1,128)} %copy.150), calls=%async_computation.2 | async-start | bytes 16384 | tf_op jit(solution)/shard_map/all_to_all | solution.py:106
  348.9 6.0 copy-start.20
  348.9 220.2 %all-to-all-start.1 = ((f32[16,1,1536,128]{3,2,1,0:T(8,128)}), f32[16,1,1536,128]{3,2,1,0:T(8,128)}, u32[]{:S(2)}, u32[]{:S(2)}) async-start(f32[16,1,1536,128]{3,2,1,0:T(8,128)} %copy.148), calls=%async_computation.1 | async-start | bytes 25165824 | tf_op jit(solution)/shard_map/all_to_all | solution.py:105
  569.1 45.6 %all-to-all-start = ((s32[4,1,8]{2,1,0:T(1,128)}), s32[4,1,8]{2,1,0:T(1,128)S(1)}, u32[]{:S(2)}, u32[]{:S(2)}) async-start(s32[4,1,8]{2,1,0:T(1,128)} %bitcast.1), calls=%async_computation | async-start | bytes 4096 | tf_op jit(solution)/shard_map/all_to_all | solution.py:127
  614.7 77.6 %slice-start = ((s8[4718592]{0:T(1024)(128)(4,1)}), s8[524288]{0:T(1024)(128)(4,1)S(1)}, s32[]{:S(2)}) async-start(s8[4718592]{0:T(1024)(128)(4,1)} %bitcast.180), calls=%async_computation.18 | async-start | bytes 1048576
  614.7 71.7 %all-to-all-start.3 = ((f32[4,8,128,384]{3,1,2,0:T(8,128)}), f32[4,8,128,384]{3,1,2,0:T(8,128)}, u32[]{:S(2)}, u32[]{:S(2)}) async-start(f32[4,8,128,384]{3,1,2,0:T(8,128)} %fusion.20), calls=%async_computation.3 | async-start | bytes 12582912 | tf_op jit(solution)/shard_map/all_to_all | solution.py:126
  620.1 190.7 %all-reduce.23.cloned.1.call-start = ((), (), s32[]{:S(2)}) async-start(), calls=%async_computation.8 | async-start | bytes 3145728 | tf_op jit(solution)/shard_map/psum | solution.py:11
  696.3 167.0 %all-reduce.25.cloned.1.call-start = ((), (), s32[]{:S(2)}) async-start(), calls=%async_computation.9 | async-start | bytes 3145728 | tf_op jit(solution)/shard_map/psum | solution.py:11
  813.5 168.8 %all-reduce.27.cloned.1.call-start = ((), (), s32[]{:S(2)}) async-start(), calls=%async_computation.10 | async-start | bytes 3145728 | tf_op jit(solution)/shard_map/psum | solution.py:11
  875.7 159.1 %all-reduce.29.cloned.1.call-start = ((), (), s32[]{:S(2)}) async-start(), calls=%async_computation.11 | async-start | bytes 3145728 | tf_op jit(solution)/shard_map/psum | solution.py:11
  985.1 168.8 %all-reduce.31.cloned.1.call-start = ((), (), s32[]{:S(2)}) async-start(), calls=%async_computation.12 | async-start | bytes 3145728 | tf_op jit(solution)/shard_map/psum | solution.py:11
  1047.2 159.1 %all-reduce.33.cloned.1.call-start = ((), (), s32[]{:S(2)}) async-start(), calls=%async_computation.13 | async-start | bytes 3145728 | tf_op jit(solution)/shard_map/psum | solution.py:11
  1156.6 168.9 %all-reduce.35.cloned.1.call-start = ((), (), s32[]{:S(2)}) async-start(), calls=%async_computation.14 | async-start | bytes 3145728 | tf_op jit(solution)/shard_map/psum | solution.py:11
  1218.8 159.2 %all-reduce.37.cloned.1.call-start = ((), (), s32[]{:S(2)}) async-start(), calls=%async_computation.15 | async-start | bytes 3145728 | tf_op jit(solution)/shard_map/psum | solution.py:11
  1328.2 168.8 %all-reduce.39.cloned.1.call-start = ((), (), s32[]{:S(2)}) async-start(), calls=%async_computation.16 | async-start | bytes 3145728 | tf_op jit(solution)/shard_map/psum | solution.py:11
  1390.4 159.2 %all-reduce.41.cloned.1.call-start = ((), (), s32[]{:S(2)}) async-start(), calls=%async_computation.17 | async-start | bytes 3145728 | tf_op jit(solution)/shard_map/psum | solution.py:11
  (17 other events, 36.7 us)
Sparse Core Ops, SparseCore 0:
  14.5 43.2 all-reduce.14
  61.5 89.8 all-reduce.16
  167.9 40.7 all-reduce.18
  211.8 89.9 all-reduce.20
  696.5 114.2 all-reduce.22
  813.6 49.6 all-reduce.24
  875.8 106.4 all-reduce.26
  985.2 49.6 all-reduce.28
  1047.4 106.4 all-reduce.30
  1156.7 49.6 all-reduce.32
  1218.9 106.5 all-reduce.34
  1328.3 49.6 all-reduce.36
  1390.5 106.4 all-reduce.38
  1499.9 49.6 all-reduce.40
where the time goes:
time: 1580 us; the launch traced here: 1570 us
  waiting for transfers between devices  1240 us (78%)
  local copies, waits for them, and re-layouts  132 us (8%)
  matrix products  126 us (8%)
  other arithmetic  34.3 us (2%)
  starting transfers between devices  19.8 us (1%)
    psum x14, waiting for transfers between devices, from_root(): return lax.psum(kept, axis)  961 us
    all_to_all x1, waiting for transfers between devices, body(): lax.all_to_all(outgoing, 'col', split_axis=0, concat_axis=0, tiled=True)  213 us
    dot_general x21, matrix products, product(): jnp.dot(first, second, precision=HIGHEST, preferred_element_type=jnp.floa...  76.8 us
    all_to_all x1, waiting for transfers between devices, body(): lax.all_to_all(row_outgoing, 'row', split_axis=0, concat_axis=0, tiled=True)  66.3 us
    another operation x10, local copies, waits for them, and re-layouts, renew(): jnp.tile(scaled_cols, (1, matrix.shape[1] // block_size))  46 us
  transfers between devices with their start and end apart: 18, of which 16 were waited for; matrix products, arithmetic and copies ran while one was open for 11% of the time, Pallas kernels for 0%

commit v1 on v0

v1 whole, which is shorter than its diff:
```python
import functools

import jax
import jax.numpy as jnp
from jax import lax
from jax.experimental import pallas as pl
from jax.experimental.pallas import tpu as pltpu
from jax.sharding import PartitionSpec as P

MESH = pl.DeviceIdType.MESH
HIGHEST = lax.Precision.HIGHEST
F32 = jnp.float32
ANY = pl.BlockSpec(memory_space=pl.ANY)
VMEM = pl.BlockSpec(memory_space=pltpu.VMEM)
SMEM = pl.BlockSpec(memory_space=pltpu.SMEM)
B = 128
PIECE = 48


def dot(a, b):
    return jnp.dot(a, b, precision=HIGHEST, preferred_element_type=F32)


def place():
    col = lax.axis_index("col")
    return lax.axis_index("front"), lax.axis_index("row"), col // 4, col % 4


def ring(i, d):
    return lax.rem(i + d + 4, 4)


def gather_kernel(panels, locals_, cross, exchange, src_ref, u_ref, w_ref, pp_ref, loc, loct, *sems):
    (ls, su, ru, ss, rs, s2, r2, s3, r3, s4, r4, s5, r5) = sems
    f, y, x, z = place()
    count = len(panels)
    own = f if cross else 0

    loads = []
    for i, take in enumerate(locals_):
        cp = pltpu.make_async_copy(take(src_ref), loc.at[i], ls.at[i])
        cp.start()
        loads.append(cp)

    barrier = pltpu.get_barrier_semaphore()
    greeted = 0
    for dy in range(4):
        for dz in range(4):
            if dy or dz:
                pl.semaphore_signal(
                    barrier, inc=1, device_id=(f, ring(y, dy), 4 * x + ring(z, dz)), device_id_type=MESH
                )
                greeted += 1
    for dx in range(1, 4):
        pl.semaphore_signal(barrier, inc=1, device_id=(f, y, 4 * ring(x, dx) + z), device_id_type=MESH)
        greeted += 1
    if cross:
        pl.semaphore_signal(barrier, inc=1, device_id=(1 - f, y, 4 * x + z), device_id_type=MESH)
        greeted += 1
    for i, cp in enumerate(loads):
        cp.wait()
        for t in range(3):
            flat = loc[i, :, t * B : (t + 1) * B].T
            for n in range(8):
                lo, hi = max(n * PIECE, t * B), min((n + 1) * PIECE, (t + 1) * B)
                if lo < hi:
                    loct[i, n // 2, n % 2, lo - n * PIECE : hi - n * PIECE, :] = flat[lo - t * B : hi - t * B]
    pl.semaphore_wait(barrier, greeted)

    def remote(src, dst, ssem, rsem, device):
        return pltpu.make_async_remote_copy(
            src_ref=src, dst_ref=dst, send_sem=ssem, recv_sem=rsem, device_id=device, device_id_type=MESH
        )

    def first(p, op):
        sy, i = panels[p]
        for zz in range(4):
            mine = (y == z) & (z == zz)
            cp = remote(loct.at[i, zz], w_ref.at[own, p, x, zz], ss.at[p, zz], rs.at[p], (f, z, 4 * x + zz))
            here = pltpu.make_async_copy(loct.at[i, zz], w_ref.at[own, p, x, zz], ss.at[p, zz])

            @pl.when(jnp.logical_not(mine))
            def _():
                cp.start() if op == "start" else cp.wait_send()

            @pl.when(mine)
            def _():
                here.start() if op == "start" else here.wait()

        for dy in range(1, 4):
            cp = remote(loc.at[i], u_ref.at[p], su.at[p, dy], ru.at[p], (f, ring(y, dy), 4 * x + z))
            cp.start() if op == "start" else cp.wait_send()
        here = pltpu.make_async_copy(loc.at[i], u_ref.at[p], su.at[p, 0])
        here.start() if op == "start" else here.wait()

    for p, (sy, i) in enumerate(panels):
        pl.when(y == sy)(functools.partial(first, p, "start"))
    for p, (sy, i) in enumerate(panels):
        pl.when(y == sy)(functools.partial(first, p, "wait"))
    for p, (sy, i) in enumerate(panels):

        @pl.when(jnp.logical_not((y == sy) & (y == z)))
        def _():
            remote(w_ref.at[own, p, x, z], w_ref.at[own, p, x, z], ss.at[p, 0], rs.at[p], (f, y, 4 * x + z)).wait_recv()

    along_x = [w_ref.at[own, :, ring(x, -d), z, 0] for d in range(4)]
    along_z = [w_ref.at[own, :, x, ring(z, -d), 1] for d in range(4)]
    sent = []
    for d in (1, 3, 2):
        cp = remote(along_x[0], along_x[0], s2.at[0, d], r2.at[0, d], (f, y, 4 * ring(x, d) + z))
        cp.start()
        sent.append(cp)
        cp = remote(along_z[0], along_z[0], s2.at[1, d], r2.at[1, d], (f, y, 4 * x + ring(z, d)))
        cp.start()
        sent.append(cp)

    def arrived(region, rsem):
        remote(region, region, s2.at[0, 0], rsem, (f, y, 4 * x + z)).wait_recv()

    other = (1 - f, y, 4 * x + z)

    def across(n, region):
        if cross:
            cp = remote(region, region, s4.at[n], r4.at[n], other)
            cp.start()
            sent.append(cp)

    for d in (1, 3, 2):
        arrived(along_x[d], r2.at[0, d])
    part_x = [w_ref.at[own, :, :, ring(z, -d), 0] for d in range(4)]
    for d in (1, 3, 2):
        cp = remote(part_x[0], part_x[0], s3.at[0, d], r3.at[0, d], (f, y, 4 * x + ring(z, d)))
        cp.start()
        sent.append(cp)
    for d in (1, 3, 2):
        arrived(along_z[d], r2.at[1, d])
    part_z = [w_ref.at[own, :, ring(x, -d), :, 1] for d in range(4)]
    for d in (1, 3, 2):
        cp = remote(part_z[0], part_z[0], s3.at[1, d], r3.at[1, d], (f, y, 4 * ring(x, d) + z))
        cp.start()
        sent.append(cp)
    across(0, part_x[0])
    across(4, part_z[0])
    for d in (1, 3, 2):
        arrived(part_x[d], r3.at[0, d])
        across(d, part_x[d])
        arrived(part_z[d], r3.at[1, d])
        across(4 + d, part_z[d])
    if cross:
        theirs_x = [w_ref.at[1 - f, :, :, ring(z, -d), 0] for d in range(4)]
        theirs_z = [w_ref.at[1 - f, :, ring(x, -d), :, 1] for d in range(4)]
        for d in range(4):
            arrived(theirs_x[d], r4.at[d])
            arrived(theirs_z[d], r4.at[4 + d])

    def couple(e, op):
        sy, base, n, m = exchange[e]
        for part, (src, dst) in enumerate(
            (
                (w_ref.at[0, 0:n, m, 0], pp_ref.at[base : base + n, 0:2]),
                (w_ref.at[0, 0:n, m, 1, 0], pp_ref.at[base : base + n, 2]),
            )
        ):
            for dy in range(1, 4):
                cp = remote(src, dst, s5.at[e, part, dy], r5.at[e, part], (f, ring(y, dy), 4 * x + z))
                cp.start() if op == "start" else cp.wait_send()
            cp = pltpu.make_async_copy(src, dst, s5.at[e, part, 0])
            cp.start() if op == "start" else cp.wait()

    for e, (sy, base, n, m) in enumerate(exchange):
        pl.when(y == sy)(functools.partial(couple, e, "start"))
    for e, (sy, base, n, m) in enumerate(exchange):

        @pl.when(y != sy)
        def _():
            arrived(pp_ref.at[base : base + n, 0:2], r5.at[e, 0])
            arrived(pp_ref.at[base : base + n, 2], r5.at[e, 1])

        pl.when(y == sy)(functools.partial(couple, e, "wait"))
    for p, (sy, i) in enumerate(panels):

        @pl.when(y != sy)
        def _():
            arrived(u_ref.at[p], ru.at[p])

    for cp in sent:
        cp.wait_send()


def gather(source, panels, locals_, cross, exchange, pairs, cid):
    count, fronts = len(panels), 2 if cross else 1
    dma = pltpu.SemaphoreType.DMA
    n = len(locals_)

    def kernel(src_ref, u_ref, w_ref, pp_ref, loc, loct, *sems):
        gather_kernel(panels, locals_, cross, exchange, src_ref, u_ref, w_ref, pp_ref, loc, loct, *sems)

    u, w, pp = pl.pallas_call(
        kernel,
        out_shape=(
            jax.ShapeDtypeStruct((count, B, 3 * B), F32),
            jax.ShapeDtypeStruct((fronts, count, 4, 4, 2, PIECE, B), F32),
            jax.ShapeDtypeStruct((pairs, 3, PIECE, B), F32),
        ),
        in_specs=[ANY],
        out_specs=(ANY, ANY, ANY),
        scratch_shapes=[
            pltpu.VMEM((n, B, 3 * B), F32),
            pltpu.VMEM((n, 4, 2, PIECE, B), F32),
            dma((n,)),
            dma((count, 4)),
            dma((count,)),
            dma((count, 4)),
            dma((count,)),
            dma((2, 4)),
            dma((2, 4)),
            dma((2, 4)),
            dma((2, 4)),
            dma((8,)),
            dma((8,)),
            dma((len(exchange), 2, 4)),
            dma((len(exchange), 2)),
        ],
        compiler_params=pltpu.CompilerParams(
            collective_id=cid, has_side_effects=True, vmem_limit_bytes=16 << 20
        ),
        name="gather_panels",
    )(source)
    return u, w.reshape(fronts, count, 4, 3 * B, B), pp.reshape(pairs, 3 * PIECE, B)


def offsets(map_ref):
    return [lax.rem(map_ref[c, 16 * t + 3] - 3 + 16, 16) for c in range(2) for t in range(3)]


def slots(offs):
    table = {}
    for r in range(4):
        first, second = jnp.int32(-1), jnp.int32(-1)
        for i, o in enumerate(offs):
            hit = lax.rem(o, 4) == r
            second = jnp.where(hit & (first >= 0), i, second)
            first = jnp.where(hit & (first < 0), i, first)
        table[r, 0], table[r, 1] = first, second
    return table


def pick(values, index):
    out = values[0]
    for i in range(1, len(values)):
        out = jnp.where(index == i, values[i], out)
    return out


def child_kernel(map_ref, f_ref, u_ref, w_ref, pp_ref, g_ref, out_ref, q_ref, l_ref):
    f, y, x, z = place()
    offs = offsets(map_ref)
    for c in range(2):
        l10 = dot(pp_ref[c, 0:B, :], g_ref[c, 0])
        l_ref[c] = l10.T
        v0 = u_ref[c]
        v1 = u_ref[2 + c] - dot(l10, v0)
        q_ref[c, 0:B, :] = dot(g_ref[c, 0], v0)
        q_ref[c, B : 2 * B, :] = dot(g_ref[c, 1], v1)
    for i in range(6):
        c, t = i // 3, i % 3
        r, q = lax.rem(offs[i], 4), offs[i] // 4
        rank = jnp.int32(0)
        for k in range(i):
            rank = rank + (lax.rem(offs[k], 4) == r).astype(jnp.int32)
        carry = (y + r) // 4
        dz = ring(lax.rem(y + r, 4), -z)

        def slab(m, _, c=c, t=t, q=q, rank=rank, carry=carry, dz=dz):
            dx = ring(lax.rem(m + q + carry, 4), -x)
            rows = pl.ds(t * B, B)
            w0 = w_ref[0, c, m, rows, :]
            w1 = w_ref[0, 2 + c, m, rows, :] - dot(w0, l_ref[c])
            full = jnp.concatenate([w0, w1], axis=1)
            out_ref[dz, rank, dx] = f_ref[c, 4 * t + m] - dot(full, q_ref[c])
            return 0

        lax.fori_loop(0, 4, slab, 0)


def child_update(block_map, fronts, u, w, pp, inverses):
    return pl.pallas_call(
        child_kernel,
        out_shape=jax.ShapeDtypeStruct((4, 2, 4, B, 3 * B), F32),
        in_specs=[SMEM, VMEM, VMEM, VMEM, VMEM, VMEM],
        out_specs=VMEM,
        scratch_shapes=[pltpu.VMEM((2, 2 * B, 3 * B), F32), pltpu.VMEM((2, B, B), F32)],
        compiler_params=pltpu.CompilerParams(vmem_limit_bytes=48 << 20),
        name="child_update",
    )(block_map, fronts.reshape(2, 12, B, 3 * B), u, w, pp, inverses)


def exchange_kernel(map_ref, in_ref, out_ref, rz, rx, sy, *sems):
    szs, szr, sxs, sxr, sys_, syr, own_sem = sems
    f, y, x, z = place()

    barrier = pltpu.get_barrier_semaphore()
    for d in range(1, 4):
        for device in (
            (f, ring(y, d), 4 * x + z),
            (f, y, 4 * ring(x, d) + z),
            (f, y, 4 * x + ring(z, d)),
        ):
            pl.semaphore_signal(barrier, inc=1, device_id=device, device_id_type=MESH)
    own = pltpu.make_async_copy(in_ref.at[0], rz.at[0], own_sem)
    own.start()
    pl.semaphore_wait(barrier, 9)

    offs = offsets(map_ref)
    table = slots(offs)
    residues = [lax.rem(o, 4) for o in offs]

    def remote(src, dst, ssem, rsem, device):
        return pltpu.make_async_remote_copy(
            src_ref=src, dst_ref=dst, send_sem=ssem, recv_sem=rsem, device_id=device, device_id_type=MESH
        )

    def z_copy(dz, s, dx):
        return remote(
            in_ref.at[dz, s, dx], rz.at[dz, s, dx], szs.at[dz, s, dx], szr.at[dz, s, dx], (f, y, 4 * x + ring(z, dz))
        )

    def x_copy(dx, dz, s):
        return remote(
            rz.at[dz, s, dx], rx.at[dx, dz, s], sxs.at[dx, dz, s], sxr.at[dx, dz, s], (f, y, 4 * ring(x, dx) + z)
        )

    def y_copy(dy, s, dx):
        return remote(
            sy.at[dy, s, dx], out_ref.at[dy, s, dx], sys_.at[dy, s, dx], syr.at[dy, s, dx], (f, ring(y, dy), 4 * x + z)
        )

    groups = [(s, dx) for s in range(2) for dx in (1, 3, 2, 0)]
    for s, dx in groups:
        for dz in (1, 3, 2):
            z_copy(dz, s, dx).start()
    own.wait()

    def pass_x(s, dx):
        for dz in (0, 1, 3, 2):
            if dz:
                z_copy(dz, s, dx).wait_recv()
            if dx:
                x_copy(dx, dz, s).start()

    def pass_y(s, dx):
        if dx:
            for dz in range(4):
                x_copy(dx, dz, s).wait_recv()
        home = ring(z, -y)
        slot = pick([table[r, s] for r in range(4)], home)
        for dy in (1, 3, 2, 0):
            for t in range(3):
                res = jnp.where(slot >= 3, residues[3 + t], residues[t])
                origin = lax.rem(ring(y, dy) - res + 4, 4)
                dz = lax.rem(z - origin + 4, 4)
                lanes = slice(t * B, (t + 1) * B)
                if dx:
                    cands = [rx[dx, k, s, :, lanes] for k in range(4)]
                else:
                    cands = [rz[k, s, 0, :, lanes] for k in range(4)]
                sy[dy, s, dx, :, lanes] = pick(cands, dz)
            if dy:
                y_copy(dy, s, dx).start()
            else:
                pltpu.make_async_copy(sy.at[0, s, dx], out_ref.at[0, s, dx], sys_.at[0, s, dx]).start()

    for n in range(len(groups) + 1):
        if n < len(groups):
            pass_x(*groups[n])
        if n:
            pass_y(*groups[n - 1])
    for s, dx in groups:
        for d in (1, 3, 2):
            z_copy(d, s, dx).wait_send()
            y_copy(d, s, dx).wait_send()
        if dx:
            for dz in range(4):
                x_copy(dx, dz, s).wait_send()
        pltpu.make_async_copy(sy.at[0, s, dx], out_ref.at[0, s, dx], sys_.at[0, s, dx]).wait()
        for d in (1, 3, 2):
            y_copy(d, s, dx).wait_recv()


def exchange(block_map, staged, cid):
    dma = pltpu.SemaphoreType.DMA
    slab = (B, 3 * B)
    return pl.pallas_call(
        exchange_kernel,
        out_shape=jax.ShapeDtypeStruct((4, 2, 4) + slab, F32),
        in_specs=[SMEM, ANY],
        out_specs=ANY,
        scratch_shapes=[
            pltpu.VMEM((4, 2, 4) + slab, F32),
            pltpu.VMEM((4, 4, 2) + slab, F32),
            pltpu.VMEM((4, 2, 4) + slab, F32),
            dma((4, 2, 4)),
            dma((4, 2, 4)),
            dma((4, 4, 2)),
            dma((4, 4, 2)),
            dma((4, 2, 4)),
            dma((4, 2, 4)),
            dma,
        ],
        compiler_params=pltpu.CompilerParams(
            collective_id=cid, has_side_effects=True, vmem_limit_bytes=40 << 20
        ),
        name="exchange",
    )(block_map, staged)


def extend_add(block_map, received, parent):
    def kernel(map_ref, in_ref, parent_ref, out_ref, acc):
        def load(u, _):
            for v in range(3):
                acc[u, v] = parent_ref[u, :, v * B : (v + 1) * B]
            return 0

        lax.fori_loop(0, 24, load, 0)
        add_body(map_ref, in_ref, acc)

        def store(u, _):
            for v in range(3):
                out_ref[u, :, v * B : (v + 1) * B] = acc[u, v]
            return 0

        lax.fori_loop(0, 24, store, 0)

    out = pl.pallas_call(
        kernel,
        out_shape=jax.ShapeDtypeStruct((24, B, 3 * B), F32),
        in_specs=[SMEM, VMEM, VMEM],
        out_specs=VMEM,
        scratch_shapes=[pltpu.VMEM((24, 3, B, B), F32)],
        compiler_params=pltpu.CompilerParams(vmem_limit_bytes=48 << 20),
        name="extend_add",
    )(block_map, received, parent.reshape(24, B, 3 * B))
    return out.reshape(24 * B, 3 * B)


def add_body(map_ref, in_ref, acc):
    f, y, x, z = place()
    offs = offsets(map_ref)
    table = slots(offs)
    for dy in range(4):
        src_y = ring(y, -dy)
        r = ring(z, -src_y)
        carry = (src_y + r) // 4
        for s in range(2):
            slot = pick([table[k, s] for k in range(4)], r)
            c = (slot >= 3).astype(jnp.int32)
            t_i = jnp.maximum(slot - 3 * c, 0)
            m = lax.rem(x - pick(offs, slot) // 4 - carry + 8, 4)
            i = 16 * t_i + 4 * m + src_y
            col_slot = map_ref[c, i] // 32
            for t in range(3):
                res = lax.rem(jnp.where(slot >= 3, offs[3 + t], offs[t]), 4)

                def step(dx, _, t=t, res=res, slot=slot, c=c, i=i, col_slot=col_slot, dy=dy, s=s):
                    j = 16 * t + 4 * ring(x, -dx) + ring(y, -res)
                    row_slot = map_ref[c, j] // 4

                    @pl.when((slot >= 0) & (i >= 2) & (j >= 2))
                    def _():
                        acc[row_slot, col_slot] += in_ref[dy, s, dx, :, t * B : (t + 1) * B].T

                    return 0

                lax.fori_loop(0, 4, step, 0)


PAIR = {(1, 0): 0, (2, 0): 1, (2, 1): 2, (3, 0): 3, (3, 1): 4, (3, 2): 5, (4, 0): 6, (4, 1): 7, (4, 2): 8, (4, 3): 9}


def parent_kernel(a_ref, u_ref, w_ref, pp_ref, g_ref, out_ref, cur, lt, v_ref, q_ref, wt):
    f, y, x, z = place()
    steps = range(5)
    for n in range(10):
        cur[n] = pp_ref[n, 0:B, :]
    for j in steps:
        v_ref[j] = u_ref[j]
    for j in range(4):
        for k in range(j + 1, 5):
            l_kj = dot(cur[PAIR[k, j]], g_ref[j])
            lt[PAIR[k, j]] = l_kj.T
            for i in range(j + 1, k):
                cur[PAIR[k, i]] -= dot(l_kj, cur[PAIR[i, j]].T)
            v_ref[k] -= dot(l_kj, v_ref[j])
    for k in steps:
        q_ref[k * B : (k + 1) * B, :] = dot(g_ref[k], v_ref[k])

    col = 4 * x + z
    pivot_col = (f == 0) & (col < 5)

    def rows(n, _):
        u, rest = n // 8, lax.rem(n, 8)
        ff, m = rest // 4, lax.rem(rest, 4)
        part = pl.ds(pl.multiple_of(u * B, B), B)
        for k in steps:
            w = w_ref[ff, k, m, part, :]
            if k:
                w = w - dot(
                    wt[:, 0 : k * B],
                    jnp.concatenate([lt[PAIR[k, j]] for j in range(k)], axis=0),
                )
            wt[:, k * B : (k + 1) * B] = w
        out_ref[n] = a_ref[n] - dot(wt[...], q_ref[...])

        @pl.when(pivot_col)
        def _():
            row = 4 * n + y
            for k in steps:

                @pl.when((col == k) & (row > k))
                def _():
                    out_ref[n, :, 0:B] = dot(wt[:, k * B : (k + 1) * B], g_ref[k])

                @pl.when((col == k) & (row == k))
                def _():
                    if k:
                        out_ref[n, :, 0:B] = a_ref[n, :, 0:B] - dot(wt[:, 0 : k * B], q_ref[0 : k * B, 0:B])
                    else:
                        out_ref[n, :, 0:B] = a_ref[n, :, 0:B]

        return 0

    lax.fori_loop(0, 24, rows, 0)
    for k in steps:

        @pl.when(y == k % 4)
        def _():
            panel = q_ref[k * B : (k + 1) * B, :]
            keep = (f == 0) & (col <= k)
            out_ref[k // 4, :, B:] = panel[:, B:]
            out_ref[k // 4, :, 0:B] = jnp.where(keep, out_ref[k // 4, :, 0:B], panel[:, 0:B])


def parent_update(a, u, w, pp, inverses):
    out = pl.pallas_call(
        parent_kernel,
        out_shape=jax.ShapeDtypeStruct((24, B, 3 * B), F32),
        in_specs=[VMEM] * 5,
        out_specs=VMEM,
        scratch_shapes=[
            pltpu.VMEM((10, B, B), F32),
            pltpu.VMEM((10, B, B), F32),
            pltpu.VMEM((5, B, 3 * B), F32),
            pltpu.VMEM((5 * B, 3 * B), F32),
            pltpu.VMEM((B, 5 * B), F32),
        ],
        compiler_params=pltpu.CompilerParams(vmem_limit_bytes=48 << 20),
        name="parent_update",
    )(a.reshape(24, B, 3 * B), u, w, pp, inverses)
    return out.reshape(24 * B, 3 * B)


CHILD_PANELS = ((0, 0), (0, 1), (1, 0), (1, 1))
PARENT_PANELS = ((0, 0), (1, 0), (2, 0), (3, 0), (0, 1))


def body(child_fronts, parent_front, child_inverses, parent_inverses, block_map):
    u, w, pp = gather(
        child_fronts,
        CHILD_PANELS,
        [lambda ref: ref.at[0, 0:B, :], lambda ref: ref.at[1, 0:B, :]],
        False,
        ((1, 0, 2, 0),),
        2,
        0,
    )
    staged = child_update(block_map, child_fronts, u, w, pp, child_inverses)
    received = exchange(block_map, staged, 1)
    a = extend_add(block_map, received, parent_front)
    u, w, pp = gather(
        a,
        PARENT_PANELS,
        [lambda ref: ref.at[0:B, :], lambda ref: ref.at[B : 2 * B, :]],
        True,
        ((1, 0, 1, 0), (2, 1, 2, 0), (3, 3, 3, 0), (0, 6, 4, 1)),
        10,
        2,
    )
    return parent_update(a, u, w, pp, parent_inverses)


def solution(mesh):
    placed = (
        P("front", "row", "col"),
        P("row", ("front", "col")),
        P("front", None, None, None),
        P(),
        P("front", None),
    )
    return jax.shard_map(
        body, mesh=mesh, in_specs=placed, out_specs=P("row", ("front", "col")), check_vma=False
    )
```

time: 1580 us -> 354 us (0.22)
  waiting for transfers between devices: 1240 us -> 0 us
  Pallas kernels: 0 us -> 338 us
  matrix products: 126 us -> 0 us
  local copies, waits for them, and re-layouts: 132 us -> 10.9 us
  other arithmetic: 34.3 us -> 0 us
  starting transfers between devices: 19.8 us -> 0 us
    psum x14 -> x0, waiting for transfers between devices: 961 us -> none  [from_root(): return lax.psum(kept, axis)]
    pallas_call x0 -> x6, Pallas kernels: none -> 338 us  [the longest x2 152 us: gather(): pl.pallas_call(kernel, out_shape=(jax.ShapeDtypeStruct((count, B, 3 * B),...]
    all_to_all x4 -> x0, waiting for transfers between devices: 279 us -> none  [the longest x1 213 us: body(): lax.all_to_all(outgoing, 'col', split_axis=0, concat_axis=0, tiled=True)]
    dot_general x25 -> x0, matrix products: 126 us -> none  [the longest x21 76.8 us: product(): jnp.dot(first, second, precision=HIGHEST, preferred_element_type=jnp.floa...]
    another operation x15 -> x0, local copies, waits for them, and re-layouts: 72.8 us -> none  [the longest x10 46 us: renew(): jnp.tile(scaled_cols, (1, matrix.shape[1] // block_size))]
    select_n x15 -> x0, other arithmetic: 27.8 us -> none  [the longest x14 27.8 us: from_root(): jnp.where(lax.axis_index(axis) == source, value, 0).astype(value.dtype)]
    all_to_all x4 -> x0, starting transfers between devices: 19.3 us -> none  [the longest x1 5.37 us: body(): lax.all_to_all(row_outgoing, 'row', split_axis=0, concat_axis=0, tiled=True)]
    dot_general x16 -> x0, local copies, waits for them, and re-layouts: 18.3 us -> none  [the longest x1 13.1 us: body(): jnp.einsum('dsct,crtb->dsrb', selector, fronts.reshape(kid_count, local_r...]
  transfers between devices with their start and end apart: 18 -> 0, of which waited for: 16 -> 0; matrix products, arithmetic and copies ran while one was open for 11% -> 0% of each run, Pallas kernels for 0% -> 0%
where the time goes in v1:
time: 354 us; the launch traced here: 349 us
  Pallas kernels  338 us (95%)
  local copies, waits for them, and re-layouts  10.9 us (3%)
    pallas_call x2, Pallas kernels, gather(): pl.pallas_call(kernel, out_shape=(jax.ShapeDtypeStruct((count, B, 3 * B),...  152 us
    pallas_call x1, Pallas kernels, exchange(): pl.pallas_call(exchange_kernel, out_shape=jax.ShapeDtypeStruct((4, 2, 4)...  99.3 us
    pallas_call x1, Pallas kernels, parent_update(): pl.pallas_call(parent_kernel, out_shape=jax.ShapeDtypeStruct((24, B, 3 *...  51.9 us
    pallas_call x1, Pallas kernels, child_update(): pl.pallas_call(child_kernel, out_shape=jax.ShapeDtypeStruct((4, 2, 4, B,...  21.4 us
    pallas_call x1, Pallas kernels, extend_add(): pl.pallas_call(kernel, out_shape=jax.ShapeDtypeStruct((24, B, 3 * B), F32...  13.6 us
    unnamed x16, local copies, waits for them, and re-layouts  10.9 us

profile of v1, /device:TPU:1, one launch (start us, length us, event | category | flops | bytes accessed | tf_op | source)
XLA Modules:
  0.0 349.2 jit_solution(4776611742971256847)
XLA Ops:
  0.0 0.0 copy-start.7
  0.0 0.0 copy-start.3
  0.0 2.3 copy-done.3
  2.4 0.0 copy-start.6
  2.4 69.4 %gather_panels.2 = (f32[4,128,384]{2,1,0:T(8,128)S(1)}, f32[1,4,4,4,2,48,128]{6,5,4,3,2,1,0:T(8,128)S(1)}, f32[2,3,48,128]{3,2,1,0:T(8,128)S(1)}) custom-call(f32[2,1536,384]{2,1,0:T(8,128)S(1)} %copy-done.3), custom_call_target="tpu_custom_call" | custom-call | tf_op jit(solution)/shard_map/gather_panels/pallas_call | solution.py:198
  71.7 0.0 copy-done.7
  71.8 0.0 copy-done.6
  71.8 21.4 %child_update.1.in_ref = f32[4,2,4,128,384]{4,3,2,1,0:T(8,128)} custom-call(s32[2,48]{1,0:T(2,128)S(1)} %copy-done.7, f32[2,12,128,384]{3,2,1,0:T(8,128)} %bitcast.9, f32[4,128,384]{2,1,0:T(8,128)S(1)} %get-tuple-element.11.u_ref, f32[1,4,4,384,128]{4,3,2,1,0:T(8,128)S(1)} %bitcast.11, f32[2,144,128]{2,1,0:T(8,128)S(1)} %bitcast.13, ...), custom_call_target="tpu_custom_call" | custom-call | tf_op jit(solution)/shard_map/child_update/pallas_call | solution.py:287
  93.2 0.0 copy-start.1
  93.2 2.8 copy-done.1
  96.0 99.3 %exchange.1.in_ref = f32[4,2,4,128,384]{4,3,2,1,0:T(8,128)S(1)} custom-call(s32[2,48]{1,0:T(2,128)S(1)} %copy-done.7, f32[4,2,4,128,384]{4,3,2,1,0:T(8,128)S(1)} %copy-done.1), custom_call_target="tpu_custom_call" | custom-call | tf_op jit(solution)/shard_map/exchange/pallas_call | solution.py:393
  195.3 0.0 copy-start.2
  195.3 2.7 copy-done.2
  198.0 13.6 %extend_add.1.a_ref = f32[24,128,384]{2,1,0:T(8,128)S(1)} custom-call(s32[2,48]{1,0:T(2,128)S(1)} %copy-done.7, f32[4,2,4,128,384]{4,3,2,1,0:T(8,128)} %copy-done.2, f32[24,128,384]{2,1,0:T(8,128)} %bitcast.14), custom_call_target="tpu_custom_call" | custom-call | tf_op jit(solution)/shard_map/extend_add/pallas_call | solution.py:434
  211.6 0.0 copy-start
  211.6 0.0 copy-start.5
  211.6 82.6 %gather_panels.3 = (f32[5,128,384]{2,1,0:T(8,128)S(1)}, f32[2,5,4,4,2,48,128]{6,5,4,3,2,1,0:T(8,128)S(1)}, f32[10,3,48,128]{3,2,1,0:T(8,128)S(1)}) custom-call(f32[3072,384]{1,0:T(8,128)S(1)} %bitcast.8), custom_call_target="tpu_custom_call" | custom-call | tf_op jit(solution)/shard_map/gather_panels/pallas_call | solution.py:198
  294.2 0.0 copy-start.4
  294.3 3.0 copy-done.4
  297.3 0.0 copy-done
  297.3 0.0 copy-done.5
  297.3 51.9 %parent_update.1 = f32[24,128,384]{2,1,0:T(8,128)} custom-call(f32[24,128,384]{2,1,0:T(8,128)} %copy-done, f32[5,128,384]{2,1,0:T(8,128)S(1)} %get-tuple-element.14.u_ref, f32[2,5,4,384,128]{4,3,2,1,0:T(8,128)} %bitcast.10, f32[10,144,128]{2,1,0:T(8,128)S(1)} %bitcast.12, f32[5,128,128]{2,1,0:T(8,128)S(1)} %copy-done.5), custom_call_target="tpu_custom_call" | custom-call | tf_op jit(solution)/shard_map/parent_update/pallas_call | solution.py:544
Async XLA Ops:
  0.0 71.7 %copy-start.7 = (s32[2,48]{1,0:T(2,128)S(1)}, s32[2,48]{1,0:T(2,128)}, u32[]{:S(2)}) copy-start(s32[2,48]{1,0:T(2,128)} %map_ref.5) | copy-start | bytes 1156
  0.0 2.4 copy-start.3
  2.4 69.4 %copy-start.6 = (f32[2,2,128,128]{3,2,1,0:T(8,128)S(1)}, f32[2,2,128,128]{3,2,1,0:T(8,128)}, u32[]{:S(2)}) copy-start(f32[2,2,128,128]{3,2,1,0:T(8,128)} %g_ref.2) | copy-start | bytes 786436
  93.2 2.8 copy-start.1
  195.3 2.7 copy-start.2
  211.6 85.7 %copy-start = (f32[24,128,384]{2,1,0:T(8,128)}, f32[24,128,384]{2,1,0:T(8,128)S(1)}, u32[]{:S(2)}) copy-start(f32[24,128,384]{2,1,0:T(8,128)S(1)} %extend_add.1.a_ref) | copy-start | bytes 14155780
  211.6 85.7 %copy-start.5 = (f32[5,128,128]{2,1,0:T(8,128)S(1)}, f32[5,128,128]{2,1,0:T(8,128)}, u32[]{:S(2)}) copy-start(f32[5,128,128]{2,1,0:T(8,128)} %g_ref.3) | copy-start | bytes 983044
  294.2 3.1 copy-start.4

commit v2 on v0

v2 whole, which is shorter than its diff:
```python
import functools

import jax
import jax.numpy as jnp
from jax import lax
from jax.experimental import pallas as pl
from jax.experimental.pallas import tpu as pltpu
from jax.sharding import PartitionSpec as P

MESH = pl.DeviceIdType.MESH
F32, BF16 = jnp.float32, jnp.bfloat16
ANY = pl.BlockSpec(memory_space=pltpu.HBM)
VMEM = pl.BlockSpec(memory_space=pltpu.VMEM)
SMEM = pl.BlockSpec(memory_space=pltpu.SMEM)
DMA = pltpu.SemaphoreType.DMA
B = 128
AROUND = (1, 3, 2)
TILE = (4, 2, 16, B)


def split(a):
    high = a.astype(BF16)
    return high, (a - high.astype(F32)).astype(BF16)


def lhs3(a):
    high, low = split(a)
    return jnp.concatenate([high, high, low], axis=1)


def rhs3(b):
    high, low = split(b)
    return jnp.concatenate([high, low, high], axis=0)


def mul3(a, b):
    return jnp.dot(a, b, preferred_element_type=F32)


def dot(a, b):
    return mul3(lhs3(a), rhs3(b))


def place():
    col = lax.axis_index("col")
    return lax.axis_index("front"), lax.axis_index("row"), col // 4, col % 4


def ring(i, d):
    return lax.rem(i + d + 4, 4)


def remote(src, dst, ssem, rsem, device):
    return pltpu.make_async_remote_copy(
        src_ref=src, dst_ref=dst, send_sem=ssem, recv_sem=rsem, device_id=device, device_id_type=MESH
    )


def pick(values, index):
    out = values[0]
    for i in range(1, len(values)):
        out = jnp.where(index == i, values[i], out)
    return out


def gather(panels, cross, couplings, loc, loct, u_ref, w_ref, pp_ref, sems, idle):
    su, ru, ss, rs, s2, r2, s3, r3, s4, r4, s5, r5 = sems
    f, y, x, z = place()
    own = f if cross else 0
    late = []

    def scatter(p, op):
        i = panels[p][1]
        for zz in range(4):
            mine = (y == z) & (z == zz)
            src, dst = loct.at[i, :, zz], w_ref.at[own, p, x, :, zz]
            cp = remote(src, dst, ss.at[p, zz], rs.at[p], (f, z, 4 * x + zz))
            here = pltpu.make_async_copy(src, dst, ss.at[p, zz])

            @pl.when(jnp.logical_not(mine))
            def _():
                cp.start() if op == "start" else cp.wait_send()

            @pl.when(mine)
            def _():
                here.start() if op == "start" else here.wait()

    def column(p, op):
        i = panels[p][1]
        for dy in AROUND:
            cp = remote(loc.at[i], u_ref.at[p], su.at[p, dy], ru.at[p], (f, ring(y, dy), 4 * x + z))
            cp.start() if op == "start" else cp.wait_send()
        here = pltpu.make_async_copy(loc.at[i], u_ref.at[p], su.at[p, 0])
        here.start() if op == "start" else here.wait()

    for step in (scatter, column):
        for p, (sy, i) in enumerate(panels):
            pl.when(y == sy)(functools.partial(step, p, "start"))
    idle(0)
    for p, (sy, i) in enumerate(panels):
        region = w_ref.at[own, p, x, :, z]

        @pl.when(jnp.logical_not((y == sy) & (y == z)))
        def _():
            remote(region, region, ss.at[p, 0], rs.at[p], (f, y, 4 * x + z)).wait_recv()

        @pl.when((y == sy) & (y == z))
        def _():
            for zz in range(4):

                @pl.when(z == zz)
                def _():
                    pltpu.make_async_copy(region, region, ss.at[p, zz]).wait()

    along_x = [w_ref.at[own, :, ring(x, -d), :, z, 0] for d in range(4)]
    along_z = [w_ref.at[own, :, x, :, ring(z, -d), 1] for d in range(4)]
    part_x = [w_ref.at[own, :, :, :, ring(z, -d), 0] for d in range(4)]
    part_z = [w_ref.at[own, :, ring(x, -d), :, :, 1] for d in range(4)]

    def send(*args):
        cp = remote(*args)
        cp.start()
        late.append(cp)

    def arrived(region, rsem):
        remote(region, region, s2.at[0, 0], rsem, (f, y, 4 * x + z)).wait_recv()

    def across(n, region):
        if cross:
            send(region, region, s4.at[n], r4.at[n], (1 - f, y, 4 * x + z))

    for d in AROUND:
        send(along_x[0], along_x[0], s2.at[0, d], r2.at[0, d], (f, y, 4 * ring(x, d) + z))
        send(along_z[0], along_z[0], s2.at[1, d], r2.at[1, d], (f, y, 4 * x + ring(z, d)))
    idle(1)
    for d in AROUND:
        arrived(along_x[d], r2.at[0, d])
    for d in AROUND:
        send(part_x[0], part_x[0], s3.at[0, d], r3.at[0, d], (f, y, 4 * x + ring(z, d)))
    for d in AROUND:
        arrived(along_z[d], r2.at[1, d])
    for d in AROUND:
        send(part_z[0], part_z[0], s3.at[1, d], r3.at[1, d], (f, y, 4 * ring(x, d) + z))
    across(0, part_x[0])
    across(4, part_z[0])
    idle(2)
    for n, d in enumerate(AROUND):
        arrived(part_x[d], r3.at[0, d])
        across(d, part_x[d])
        arrived(part_z[d], r3.at[1, d])
        across(4 + d, part_z[d])
    if cross:
        for d in range(4):
            arrived(w_ref.at[1 - f, :, :, :, ring(z, -d), 0], r4.at[d])
            arrived(w_ref.at[1 - f, :, ring(x, -d), :, :, 1], r4.at[4 + d])

    def couple(e, op):
        sy, base, n, m = couplings[e]
        src, dst = w_ref.at[0, 0:n, m, 0], pp_ref.at[base : base + n]
        for dy in AROUND:
            cp = remote(src, dst, s5.at[e, dy], r5.at[e], (f, ring(y, dy), 4 * x + z))
            cp.start() if op == "start" else cp.wait_send()
        here = pltpu.make_async_copy(src, dst, s5.at[e, 0])
        here.start() if op == "start" else here.wait()

    for e, (sy, base, n, m) in enumerate(couplings):
        pl.when(y == sy)(functools.partial(couple, e, "start"))
    for p, (sy, i) in enumerate(panels):

        @pl.when(y != sy)
        def _():
            arrived(u_ref.at[p], ru.at[p])

    for e, (sy, base, n, m) in enumerate(couplings):

        @pl.when(y != sy)
        def _():
            arrived(pp_ref.at[base : base + n], r5.at[e])

        pl.when(y == sy)(functools.partial(couple, e, "wait"))

    def finish():
        def scatter_rest(p):
            i = panels[p][1]
            for zz in range(4):

                @pl.when(jnp.logical_not((y == z) & (z == zz)))
                def _():
                    src, dst = loct.at[i, :, zz], w_ref.at[own, p, x, :, zz]
                    remote(src, dst, ss.at[p, zz], rs.at[p], (f, z, 4 * x + zz)).wait_send()

        for p, (sy, i) in enumerate(panels):
            pl.when(y == sy)(functools.partial(scatter_rest, p))
        for cp in late:
            cp.wait_send()

    for p, (sy, i) in enumerate(panels):
        pl.when(y == sy)(functools.partial(column, p, "wait"))
    return finish


def gather_sems(count, couplings):
    return [
        DMA((count, 4)),
        DMA((count,)),
        DMA((count, 4)),
        DMA((count,)),
        DMA((2, 4)),
        DMA((2, 4)),
        DMA((2, 4)),
        DMA((2, 4)),
        DMA((8,)),
        DMA((8,)),
        DMA((couplings, 4)),
        DMA((couplings,)),
    ]


CHILD_PANELS = ((0, 0), (0, 1), (1, 0), (1, 1))
PARENT_PANELS = ((0, 0), (1, 0), (2, 0), (3, 0), (0, 1))
CHILD_COUPLINGS = ((1, 0, 2, 0),)
PARENT_COUPLINGS = ((1, 0, 1, 0), (2, 1, 2, 0), (3, 3, 3, 0), (0, 6, 4, 1))
PAIR = {(1, 0): 0, (2, 0): 1, (2, 1): 2, (3, 0): 3, (3, 1): 4, (3, 2): 5, (4, 0): 6, (4, 1): 7, (4, 2): 8, (4, 3): 9}


def assemble_kernel(
    map_ref, child_ref, parent_ref, ginv_ref, a_ref, u2, w2, pp2,
    fr, acc, loct, u1, w1, pp1, lt, qcat, stg, hop, fin, sy, got, load_sem, h1s, h1r, h2s, h2r, ys, yr, *sems
):
    f, y, x, z = place()
    here = (f, y, 4 * x + z)

    loads = [
        pltpu.make_async_copy(child_ref.at[:, 0:1], fr.at[:, 0:1], load_sem.at[0]),
        pltpu.make_async_copy(child_ref.at[:, 1:12], fr.at[:, 1:12], load_sem.at[1]),
        pltpu.make_async_copy(parent_ref, acc, load_sem.at[2]),
    ]
    for cp in loads:
        cp.start()

    barrier = pltpu.get_barrier_semaphore()
    greeted = []
    for dy in range(4):
        for dz in range(4):
            if dy or dz:
                greeted.append((f, ring(y, dy), 4 * x + ring(z, dz)))
    for dx in range(1, 4):
        greeted.append((f, y, 4 * ring(x, dx) + z))
    greeted.append((1 - f, y, 4 * x + z))
    for device in greeted:
        pl.semaphore_signal(barrier, inc=1, device_id=device, device_id_type=MESH)

    def turned(block):
        return block.T.reshape(TILE)

    offs = [lax.rem(map_ref[c, 16 * t + 3] - 3 + 16, 16) for c in range(2) for t in range(3)]
    residues = [lax.rem(o, 4) for o in offs]
    ranks = []
    for i in range(6):
        rank = jnp.int32(0)
        for k in range(i):
            rank = rank + (residues[k] == residues[i]).astype(jnp.int32)
        ranks.append(rank)

    def slot_of(r, s):
        slot = jnp.int32(-1)
        for i in range(6):
            slot = jnp.where((residues[i] == r) & (ranks[i] == s), i, slot)
        return slot

    loads[0].wait()
    for c in range(2):
        for t in range(3):
            loct[c, t] = turned(fr[c, 0, :, t * B : (t + 1) * B])
    pl.semaphore_wait(barrier, len(greeted))

    first_rows = fr.at[:, 0]
    finish1 = gather(
        CHILD_PANELS, False, CHILD_COUPLINGS, first_rows, loct, u1, w1, pp1, sems[0:12], lambda n: None
    )

    for c in range(2):
        l10 = dot(pp1[c].reshape(B, B), ginv_ref[c, 0])
        lt[c] = rhs3(l10.T)
        v0 = u1[c]
        v1 = u1[2 + c] - dot(l10, v0)
        qcat[c] = rhs3(jnp.concatenate([dot(ginv_ref[c, 0], v0), dot(ginv_ref[c, 1], v1)], axis=0))
    loads[1].wait()

    def slab(dz, s, dx):
        r = ring(ring(z, dz), -y)
        slot = slot_of(r, s)
        c = (slot >= 3).astype(jnp.int32)
        t = jnp.maximum(slot - 3 * c, 0)
        m = lax.rem(x + dx - pick(offs, slot) // 4 - (y + r) // 4 + 8, 4)
        w0 = w1[0, c, m, t].reshape(B, B)
        wb = w1[0, 2 + c, m, t].reshape(B, B) - mul3(lhs3(w0), lt[c])
        full = jnp.concatenate([w0, wb], axis=1)
        return fr[c, 4 * t + m] - mul3(lhs3(full), qcat[c])

    def z_device(dz):
        return (f, y, 4 * x + ring(z, dz))

    def x_device(dx):
        return (f, y, 4 * ring(x, dx) + z)

    def first(s, dz, dx):
        sem = (h1s.at[s, dz, dx], h1r.at[s, dz, dx])
        src = stg.at[s, dz, dx]
        if dz and (s == 0 or not dx):
            dst = hop.at[s, dz, dx] if dx else fin.at[s, dx, dz]
            return remote(src, dst, *sem, z_device(dz))
        dst = hop.at[s, dz, dx] if dz else fin.at[s, dx, dz]
        return remote(src, dst, *sem, x_device(dx))

    def second(s, dz, dx):
        sem = (h2s.at[s, dz, dx], h2r.at[s, dz, dx])
        device = x_device(dx) if s == 0 else z_device(dz)
        return remote(hop.at[s, dz, dx], fin.at[s, dx, dz], *sem, device)

    def begin(s, dz, dx):
        if not (dz or dx):
            fin[s, 0, 0] = slab(0, s, 0)
            return
        stg[s, dz, dx] = slab(dz, s, dx)
        first(s, dz, dx).start()

    order = [(0, 0, 0)] + [(0, dz, 0) for dz in AROUND]
    for d in AROUND:
        order += [(1, d, dx) for dx in AROUND]
        order += [(0, dz, d) for dz in AROUND]
    order += [(1, 0, 0)]
    for d in AROUND:
        order += [(1, 0, d), (0, 0, d), (1, d, 0)]
    for item in order:
        begin(*item)

    def pass_y(s, dx):
        for dz in range(4):
            if dz and dx:
                second(s, dz, dx).wait_recv()
            elif dz or dx:
                first(s, dz, dx).wait_recv()
        slot = slot_of(ring(z, -y), s)
        for dy in (1, 3, 2, 0):
            for t in range(3):
                res = jnp.where(slot >= 3, residues[3 + t], residues[t])
                dz = lax.rem(z - ring(y, dy) + res + 8, 4)
                block = pick([fin[s, dx, k, :, t * B : (t + 1) * B] for k in range(4)], dz)
                if dy:
                    sy[dy, s, dx, t] = block
                else:
                    got[0, s, dx, t] = block
            if dy:
                y_copy(dy, s, dx).start()

    def y_copy(dy, s, dx):
        return remote(
            sy.at[dy, s, dx], got.at[dy, s, dx], ys.at[dy, s, dx], yr.at[dy, s, dx], (f, ring(y, dy), 4 * x + z)
        )

    def forward(s, d):
        for e in AROUND:
            dz, dx = (e, d) if s == 0 else (d, e)
            first(s, dz, dx).wait_recv()
            second(s, dz, dx).start()

    forward(1, 1)
    pass_y(0, 0)
    forward(0, 1)
    forward(1, 3)
    forward(0, 3)
    forward(1, 2)
    forward(0, 2)
    pass_y(1, 0)
    for dx in AROUND:
        pass_y(0, dx)
        pass_y(1, dx)
    for s in range(2):
        for dx in range(4):
            for dy in AROUND:
                y_copy(dy, s, dx).wait_recv()

    loads[2].wait()

    def landing(c, target):
        block, found = jnp.int32(0), jnp.bool_(False)
        for t in range(3):
            j = 16 * t + lax.rem(target - offs[3 * c + t] + 96 * 16, 16)
            hit = map_ref[c, j] == target
            block = jnp.where(hit, j, block)
            found = found | hit
        return block, found

    col_hits = [[landing(c, 32 * v + 16 * f + 4 * x + z) for v in range(3)] for c in range(2)]

    def add_row(u):
        for c in range(2):
            j, row_found = landing(c, 4 * u + y)
            dx = lax.rem(x - lax.rem(j, 16) // 4 + 4, 4)
            t_j = j // 16
            for v in range(3):
                i, col_found = col_hits[c][v]
                dy = lax.rem(y - lax.rem(i, 4) + 4, 4)
                s = jnp.minimum(pick(ranks[3 * c : 3 * c + 3], i // 16), 1)
                block = got[dy, s, dx, t_j]
                lanes = slice(v * B, (v + 1) * B)
                acc[u, :, lanes] += jnp.where(row_found & col_found, block, 0.0).T

    def add_rows(low, high):
        def step(u, _):
            add_row(u)
            return 0

        lax.fori_loop(low, high, step, 0)

    add_rows(0, 2)
    for i in range(2):
        for t in range(3):
            loct[2 + i, t] = turned(acc[i, :, t * B : (t + 1) * B])

    bounds = [(2, 5), (5, 8), (8, 24)]
    finish2 = gather(
        PARENT_PANELS, True, PARENT_COUPLINGS, acc, loct.at[2:4], u2, w2, pp2, sems[12:24],
        lambda n: add_rows(*bounds[n]),
    )
    store = pltpu.make_async_copy(acc, a_ref, load_sem.at[0])
    store.start()
    finish1()
    finish2()
    for s in range(2):
        for dz in range(4):
            for dx in range(4):
                if dz or dx:
                    first(s, dz, dx).wait_send()
                if dz and dx:
                    second(s, dz, dx).wait_send()
        for dx in range(4):
            for dy in AROUND:
                y_copy(dy, s, dx).wait_send()
    store.wait()


def assemble(block_map, children, parent, inverses):
    slab = (B, 3 * B)
    return pl.pallas_call(
        assemble_kernel,
        out_shape=(
            jax.ShapeDtypeStruct((24,) + slab, F32),
            jax.ShapeDtypeStruct((5,) + slab, F32),
            jax.ShapeDtypeStruct((2, 5, 4, 3) + TILE, F32),
            jax.ShapeDtypeStruct((10,) + TILE, F32),
        ),
        in_specs=[SMEM, ANY, ANY, VMEM],
        out_specs=(ANY, ANY, ANY, ANY),
        scratch_shapes=[
            pltpu.VMEM((2, 12) + slab, F32),
            pltpu.VMEM((24,) + slab, F32),
            pltpu.VMEM((4, 3) + TILE, F32),
            pltpu.VMEM((4,) + slab, F32),
            pltpu.VMEM((1, 4, 4, 3) + TILE, F32),
            pltpu.VMEM((2,) + TILE, F32),
            pltpu.VMEM((2, 3 * B, B), BF16),
            pltpu.VMEM((2, 6 * B, 3 * B), BF16),
            pltpu.VMEM((2, 4, 4) + slab, F32),
            pltpu.VMEM((2, 4, 4) + slab, F32),
            pltpu.VMEM((2, 4, 4) + slab, F32),
            pltpu.VMEM((4, 2, 4, 3, B, B), F32),
            pltpu.VMEM((4, 2, 4, 3, B, B), F32),
            DMA((3,)),
            DMA((2, 4, 4)),
            DMA((2, 4, 4)),
            DMA((2, 4, 4)),
            DMA((2, 4, 4)),
            DMA((4, 2, 4)),
            DMA((4, 2, 4)),
        ]
        + gather_sems(4, 1)
        + gather_sems(5, 4),
        compiler_params=pltpu.CompilerParams(
            collective_id=0, has_side_effects=True, vmem_limit_bytes=58 << 20
        ),
        name="assemble",
    )(block_map, children.reshape((2, 12) + slab), parent.reshape((24,) + slab), inverses)


def parent_kernel(a_ref, u_ref, w_ref, pp_ref, g_ref, out_ref, cur, ltc, v_ref, q_ref, qcat, gcat, wt):
    f, y, x, z = place()
    steps = range(5)
    col = 4 * x + z
    n = pl.program_id(0)

    @pl.when(n == 0)
    def _():
        for k in range(10):
            cur[k] = pp_ref[k].reshape(B, B)
        for j in steps:
            v_ref[j] = u_ref[j]
        for j in range(4):
            for k in range(j + 1, 5):
                l_kj = dot(cur[PAIR[k, j]], g_ref[j])
                ltc[PAIR[k, j]] = l_kj.T
                for i in range(j + 1, k):
                    cur[PAIR[k, i]] -= dot(l_kj, cur[PAIR[i, j]].T)
                v_ref[k] -= dot(l_kj, v_ref[j])
        for k in steps:
            q_ref[k * B : (k + 1) * B, :] = dot(g_ref[k], v_ref[k])
            gcat[k] = rhs3(g_ref[k])
        qcat[...] = rhs3(q_ref[...])

    for k in steps:
        w = w_ref[0, k, :, 0].reshape(4 * B, B)
        if k:
            low = jnp.concatenate([ltc[PAIR[k, j]] for j in range(k)], axis=0)
            w = w - dot(wt[:, 0 : k * B], low)
        wt[:, k * B : (k + 1) * B] = w
    out = a_ref[...].reshape(4 * B, 3 * B) - mul3(lhs3(wt[...]), qcat[...])
    out_ref[...] = out.reshape(4, B, 3 * B)

    @pl.when((f == 0) & (col < 5))
    def _():
        for k in steps:

            @pl.when(col == k)
            def _():
                scaled = mul3(lhs3(wt[:, k * B : (k + 1) * B]), gcat[k])
                for i in range(4):
                    slot = 4 * n + i
                    row = 4 * slot + y

                    @pl.when(row > k)
                    def _():
                        out_ref[i, :, 0:B] = scaled[i * B : (i + 1) * B, :]

                    @pl.when(row == k)
                    def _():
                        out_ref[i, :, 0:B] = v_ref[k, :, 0:B]

    @pl.when(n == 0)
    def _():
        for k in steps:

            @pl.when(y == k % 4)
            def _():
                panel = q_ref[k * B : (k + 1) * B, :]
                keep = (f == 0) & (col <= k)
                out_ref[k // 4, :, B:] = panel[:, B:]
                out_ref[k // 4, :, 0:B] = jnp.where(keep, out_ref[k // 4, :, 0:B], panel[:, 0:B])


def parent_update(a, u, w, pp, inverses):
    def whole(shape):
        return pl.BlockSpec(shape, lambda n: (0,) * len(shape))

    return pl.pallas_call(
        parent_kernel,
        out_shape=jax.ShapeDtypeStruct((24, B, 3 * B), F32),
        grid=(6,),
        in_specs=[
            pl.BlockSpec((4, B, 3 * B), lambda n: (n, 0, 0)),
            whole((5, B, 3 * B)),
            pl.BlockSpec((1, 5, 4, 1) + TILE, lambda n: (n % 2, 0, 0, n // 2, 0, 0, 0, 0)),
            whole((10,) + TILE),
            whole((5, B, B)),
        ],
        out_specs=pl.BlockSpec((4, B, 3 * B), lambda n: (n, 0, 0)),
        scratch_shapes=[
            pltpu.VMEM((10, B, B), F32),
            pltpu.VMEM((10, B, B), F32),
            pltpu.VMEM((5, B, 3 * B), F32),
            pltpu.VMEM((5 * B, 3 * B), F32),
            pltpu.VMEM((15 * B, 3 * B), BF16),
            pltpu.VMEM((5, 3 * B, B), BF16),
            pltpu.VMEM((4 * B, 5 * B), F32),
        ],
        compiler_params=pltpu.CompilerParams(vmem_limit_bytes=48 << 20),
        name="parent_update",
    )(a, u, w, pp, inverses)


def body(child_fronts, parent_front, child_inverses, parent_inverses, block_map):
    a, u, w, pp = assemble(block_map, child_fronts, parent_front, child_inverses)
    return parent_update(a, u, w, pp, parent_inverses).reshape(parent_front.shape)


def solution(mesh):
    placed = (
        P("front", "row", "col"),
        P("row", ("front", "col")),
        P("front", None, None, None),
        P(),
        P("front", None),
    )
    return jax.shard_map(
        body, mesh=mesh, in_specs=placed, out_specs=P("row", ("front", "col")), check_vma=False
    )
```

time: 1580 us -> 253 us (0.16)
  waiting for transfers between devices: 1240 us -> 0 us
  Pallas kernels: 0 us -> 250 us
  local copies, waits for them, and re-layouts: 132 us -> 2.29 us
  matrix products: 126 us -> 0 us
  other arithmetic: 34.3 us -> 0 us
  starting transfers between devices: 19.8 us -> 0 us
    psum x14 -> x0, waiting for transfers between devices: 961 us -> none  [from_root(): return lax.psum(kept, axis)]
    all_to_all x4 -> x0, waiting for transfers between devices: 279 us -> none  [the longest x1 213 us: body(): lax.all_to_all(outgoing, 'col', split_axis=0, concat_axis=0, tiled=True)]
    pallas_call x0 -> x2, Pallas kernels: none -> 250 us  [the longest x1 227 us: assemble(): pl.pallas_call(assemble_kernel, out_shape=(jax.ShapeDtypeStruct((24,) + s...]
    dot_general x25 -> x0, matrix products: 126 us -> none  [the longest x21 76.8 us: product(): jnp.dot(first, second, precision=HIGHEST, preferred_element_type=jnp.floa...]
    another operation x15 -> x0, local copies, waits for them, and re-layouts: 72.8 us -> none  [the longest x10 46 us: renew(): jnp.tile(scaled_cols, (1, matrix.shape[1] // block_size))]
    select_n x15 -> x0, other arithmetic: 27.8 us -> none  [the longest x14 27.8 us: from_root(): jnp.where(lax.axis_index(axis) == source, value, 0).astype(value.dtype)]
    unnamed x47 -> x6, local copies, waits for them, and re-layouts: 27.1 us -> 2.29 us
    all_to_all x4 -> x0, starting transfers between devices: 19.3 us -> none  [the longest x1 5.37 us: body(): lax.all_to_all(row_outgoing, 'row', split_axis=0, concat_axis=0, tiled=True)]
  transfers between devices with their start and end apart: 18 -> 0, of which waited for: 16 -> 0; matrix products, arithmetic and copies ran while one was open for 11% -> 0% of each run, Pallas kernels for 0% -> 0%
where the time goes in v2:
time: 253 us; the launch traced here: 252 us
  Pallas kernels  250 us (99%)
    pallas_call x1, Pallas kernels, assemble(): pl.pallas_call(assemble_kernel, out_shape=(jax.ShapeDtypeStruct((24,) + s...  227 us
    pallas_call x1, Pallas kernels, parent_update(): pl.pallas_call(parent_kernel, out_shape=jax.ShapeDtypeStruct((24, B, 3 *...  22.7 us

profile of v2, /device:TPU:1, one launch (start us, length us, event | category | flops | bytes accessed | tf_op | source)
XLA Modules:
  0.0 252.4 jit_solution(283140445305421227)
XLA Ops:
  0.0 0.0 copy-start.2
  0.0 227.3 %assemble.1 = (f32[24,128,384]{2,1,0:T(8,128)}, f32[5,128,384]{2,1,0:T(8,128)}, f32[2,5,4,3,4,2,16,128]{7,6,5,4,3,2,1,0:T(8,128)}, f32[10,4,2,16,128]{4,3,2,1,0:T(8,128)}) custom-call(s32[2,48]{1,0:T(2,128)} %map_ref.1, f32[2,12,128,384]{3,2,1,0:T(8,128)} %bitcast.3, f32[24,128,384]{2,1,0:T(8,128)} %bitcast.4, f32[2,2,128,128]{3,2,1,0:T(8,128)} %ginv_ref.1), custom_call_target="tpu_custom_call" | custom-call | tf_op jit(solution)/shard_map/assemble/pallas_call | solution.py:446
  227.3 0.0 copy-done.2
  227.3 0.0 copy-start
  227.4 1.2 copy-done
  228.6 0.0 copy-start.1
  228.6 1.1 copy-done.1
  229.6 22.7 %parent_update.1 = f32[24,128,384]{2,1,0:T(8,128)} custom-call(f32[24,128,384]{2,1,0:T(8,128)} %get-tuple-element.9.a_ref, f32[5,128,384]{2,1,0:T(8,128)S(1)} %copy-done, f32[2,5,4,3,4,2,16,128]{7,6,5,4,3,2,1,0:T(8,128)} %get-tuple-element.11.w_ref, f32[10,4,2,16,128]{4,3,2,1,0:T(8,128)S(1)} %copy-done.1, f32[5,128,128]{2,1,0:T(8,128)S(1)} %copy-done.2), custom_call_target="tpu_custom_call" | custom-call | tf_op jit(solution)/shard_map/parent_update/pallas_call | solution.py:555
Async XLA Ops:
  0.0 227.3 %copy-start.2 = (f32[5,128,128]{2,1,0:T(8,128)S(1)}, f32[5,128,128]{2,1,0:T(8,128)}, u32[]{:S(2)}) copy-start(f32[5,128,128]{2,1,0:T(8,128)} %g_ref.1) | copy-start | bytes 983044
  227.3 1.2 copy-start
  228.6 1.1 copy-start.1

commit v3 on v2

--- a/solution.py
+++ b/solution.py
@@ -15,6 +15,7 @@
 DMA = pltpu.SemaphoreType.DMA
 B = 128
 AROUND = (1, 3, 2)
+HALF = 64
 TILE = (4, 2, 16, B)
 
 
@@ -67,6 +68,7 @@
     su, ru, ss, rs, s2, r2, s3, r3, s4, r4, s5, r5 = sems
     f, y, x, z = place()
     own = f if cross else 0
+    parts = (slice(0, 1), slice(1, 3)) if cross else (slice(0, 3),)
     late = []
 
     def scatter(p, op):
@@ -93,9 +95,8 @@
         here = pltpu.make_async_copy(loc.at[i], u_ref.at[p], su.at[p, 0])
         here.start() if op == "start" else here.wait()
 
-    for step in (scatter, column):
-        for p, (sy, i) in enumerate(panels):
-            pl.when(y == sy)(functools.partial(step, p, "start"))
+    for p, (sy, i) in enumerate(panels):
+        pl.when(y == sy)(functools.partial(scatter, p, "start"))
     idle(0)
     for p, (sy, i) in enumerate(panels):
         region = w_ref.at[own, p, x, :, z]
@@ -114,8 +115,12 @@
 
     along_x = [w_ref.at[own, :, ring(x, -d), :, z, 0] for d in range(4)]
     along_z = [w_ref.at[own, :, x, :, ring(z, -d), 1] for d in range(4)]
-    part_x = [w_ref.at[own, :, :, :, ring(z, -d), 0] for d in range(4)]
-    part_z = [w_ref.at[own, :, ring(x, -d), :, :, 1] for d in range(4)]
+
+    def part_x(d, ts, front=own):
+        return w_ref.at[front, :, :, ts, ring(z, -d), 0]
+
+    def part_z(d, ts, front=own):
+        return w_ref.at[front, :, ring(x, -d), ts, :, 1]
 
     def send(*args):
         cp = remote(*args)
@@ -125,59 +130,93 @@
     def arrived(region, rsem):
         remote(region, region, s2.at[0, 0], rsem, (f, y, 4 * x + z)).wait_recv()
 
-    def across(n, region):
+    def across(q, n, region):
         if cross:
-            send(region, region, s4.at[n], r4.at[n], (1 - f, y, 4 * x + z))
+            send(region, region, s4.at[q, n], r4.at[q, n], (1 - f, y, 4 * x + z))
 
     for d in AROUND:
         send(along_x[0], along_x[0], s2.at[0, d], r2.at[0, d], (f, y, 4 * ring(x, d) + z))
         send(along_z[0], along_z[0], s2.at[1, d], r2.at[1, d], (f, y, 4 * x + ring(z, d)))
+    for p, (sy, i) in enumerate(panels):
+        pl.when(y == sy)(functools.partial(column, p, "start"))
     idle(1)
     for d in AROUND:
         arrived(along_x[d], r2.at[0, d])
-    for d in AROUND:
-        send(part_x[0], part_x[0], s3.at[0, d], r3.at[0, d], (f, y, 4 * x + ring(z, d)))
+    for q, ts in enumerate(parts):
+        for d in AROUND:
+            region = part_x(0, ts)
+            send(region, region, s3.at[0, q, d], r3.at[0, q, d], (f, y, 4 * x + ring(z, d)))
     for d in AROUND:
         arrived(along_z[d], r2.at[1, d])
-    for d in AROUND:
-        send(part_z[0], part_z[0], s3.at[1, d], r3.at[1, d], (f, y, 4 * ring(x, d) + z))
-    across(0, part_x[0])
-    across(4, part_z[0])
+    for q, ts in enumerate(parts):
+        for d in AROUND:
+            region = part_z(0, ts)
+            send(region, region, s3.at[1, q, d], r3.at[1, q, d], (f, y, 4 * ring(x, d) + z))
+    for q, ts in enumerate(parts):
+        across(q, 0, part_x(0, ts))
+        across(q, 4, part_z(0, ts))
     idle(2)
-    for n, d in enumerate(AROUND):
-        arrived(part_x[d], r3.at[0, d])
-        across(d, part_x[d])
-        arrived(part_z[d], r3.at[1, d])
-        across(4 + d, part_z[d])
+
+    def collect(q, ts):
+        for d in AROUND:
+            arrived(part_x(d, ts), r3.at[0, q, d])
+            across(q, d, part_x(d, ts))
+            arrived(part_z(d, ts), r3.at[1, q, d])
+            across(q, 4 + d, part_z(d, ts))
+
+    collect(0, parts[0])
     if cross:
-        for d in range(4):
-            arrived(w_ref.at[1 - f, :, :, :, ring(z, -d), 0], r4.at[d])
-            arrived(w_ref.at[1 - f, :, ring(x, -d), :, :, 1], r4.at[4 + d])
-
-    def couple(e, op):
-        sy, base, n, m = couplings[e]
-        src, dst = w_ref.at[0, 0:n, m, 0], pp_ref.at[base : base + n]
-        for dy in AROUND:
-            cp = remote(src, dst, s5.at[e, dy], r5.at[e], (f, ring(y, dy), 4 * x + z))
-            cp.start() if op == "start" else cp.wait_send()
-        here = pltpu.make_async_copy(src, dst, s5.at[e, 0])
-        here.start() if op == "start" else here.wait()
-
-    for e, (sy, base, n, m) in enumerate(couplings):
-        pl.when(y == sy)(functools.partial(couple, e, "start"))
+
+        def couple(e, op):
+            sy, base, n, m = couplings[e]
+            src, dst = w_ref.at[0, 0:n, m, 0], pp_ref.at[base : base + n]
+            for dy in AROUND:
+                cp = remote(src, dst, s5.at[e, dy], r5.at[e], (f, ring(y, dy), 4 * x + z))
+                cp.start() if op == "start" else cp.wait_send()
+            here = pltpu.make_async_copy(src, dst, s5.at[e, 0])
+            here.start() if op == "start" else here.wait()
+
+        pair = remote(pp_ref, pp_ref, s4.at[0, 8], r4.at[0, 8], (1 - f, y, 4 * x + z))
+
+        @pl.when(f == 0)
+        def _():
+            for e, (sy, base, n, m) in enumerate(couplings):
+                pl.when(y == sy)(functools.partial(couple, e, "start"))
+
+    for q in range(1, len(parts)):
+        collect(q, parts[q])
+    if cross:
+
+        @pl.when(f == 0)
+        def _():
+            for e, (sy, base, n, m) in enumerate(couplings):
+
+                @pl.when(y != sy)
+                def _():
+                    arrived(pp_ref.at[base : base + n], r5.at[e])
+
+                pl.when(y == sy)(functools.partial(couple, e, "wait"))
+            pair.start()
+
     for p, (sy, i) in enumerate(panels):
 
         @pl.when(y != sy)
         def _():
             arrived(u_ref.at[p], ru.at[p])
 
-    for e, (sy, base, n, m) in enumerate(couplings):
-
-        @pl.when(y != sy)
+    if cross:
+        for q, ts in enumerate(parts):
+            for d in range(4):
+                arrived(part_x(d, ts, 1 - f), r4.at[q, d])
+                arrived(part_z(d, ts, 1 - f), r4.at[q, 4 + d])
+
+        @pl.when(f == 0)
         def _():
-            arrived(pp_ref.at[base : base + n], r5.at[e])
-
-        pl.when(y == sy)(functools.partial(couple, e, "wait"))
+            pair.wait_send()
+
+        @pl.when(f == 1)
+        def _():
+            pair.wait_recv()
 
     def finish():
         def scatter_rest(p):
@@ -207,10 +246,10 @@
         DMA((count,)),
         DMA((2, 4)),
         DMA((2, 4)),
-        DMA((2, 4)),
-        DMA((2, 4)),
-        DMA((8,)),
-        DMA((8,)),
+        DMA((2, 2, 4)),
+        DMA((2, 2, 4)),
+        DMA((2, 9)),
+        DMA((2, 9)),
         DMA((couplings, 4)),
         DMA((couplings,)),
     ]
@@ -218,14 +257,13 @@
 
 CHILD_PANELS = ((0, 0), (0, 1), (1, 0), (1, 1))
 PARENT_PANELS = ((0, 0), (1, 0), (2, 0), (3, 0), (0, 1))
-CHILD_COUPLINGS = ((1, 0, 2, 0),)
 PARENT_COUPLINGS = ((1, 0, 1, 0), (2, 1, 2, 0), (3, 3, 3, 0), (0, 6, 4, 1))
 PAIR = {(1, 0): 0, (2, 0): 1, (2, 1): 2, (3, 0): 3, (3, 1): 4, (3, 2): 5, (4, 0): 6, (4, 1): 7, (4, 2): 8, (4, 3): 9}
 
 
 def assemble_kernel(
     map_ref, child_ref, parent_ref, ginv_ref, a_ref, u2, w2, pp2,
-    fr, acc, loct, u1, w1, pp1, lt, qcat, stg, hop, fin, sy, got, load_sem, h1s, h1r, h2s, h2r, ys, yr, *sems
+    fr, acc, loct, u1, w1, pp1, lt, qcat, stg, hop, fin, sy, got, load_sem, tree_s, tree_r, h1s, h1r, h2s, h2r, ys, yr, *sems
 ):
     f, y, x, z = place()
     here = (f, y, 4 * x + z)
@@ -275,12 +313,73 @@
     pl.semaphore_wait(barrier, len(greeted))
 
     first_rows = fr.at[:, 0]
-    finish1 = gather(
-        CHILD_PANELS, False, CHILD_COUPLINGS, first_rows, loct, u1, w1, pp1, sems[0:12], lambda n: None
-    )
+
+    def tree_y(op):
+        src = fr.at[:, 0, :, 0:B]
+        for dy in AROUND:
+            cp = remote(src, pp1, tree_s.at[0, dy], tree_r.at[0], (f, ring(y, dy), 4 * x + z))
+            cp.start() if op == "start" else cp.wait_send()
+        cp = pltpu.make_async_copy(src, pp1, tree_s.at[0, 0])
+        cp.start() if op == "start" else cp.wait()
+
+    def tree(axis, op):
+        for d in AROUND:
+            device = (f, y, 4 * ring(x, d) + z) if axis == 1 else (f, y, 4 * x + ring(z, d))
+            cp = remote(pp1, pp1, tree_s.at[axis, d], tree_r.at[axis], device)
+            cp.start() if op == "start" else cp.wait_send()
+
+    def tree_wait(axis):
+        remote(pp1, pp1, tree_s.at[axis, 0], tree_r.at[axis], here).wait_recv()
+
+    root, line, floor = (y == 1) & (x == 0) & (z == 0), (x == 0) & (z == 0), z == 0
+
+    def couple_child(n):
+        if n == 0:
+
+            @pl.when(root)
+            def _():
+                tree_y("start")
+
+        if n == 1:
+
+            @pl.when(root)
+            def _():
+                tree_y("wait")
+
+            @pl.when(line & jnp.logical_not(root))
+            def _():
+                tree_wait(0)
+
+            @pl.when(line)
+            def _():
+                tree(1, "start")
+
+        if n == 2:
+
+            @pl.when(floor & jnp.logical_not(line))
+            def _():
+                tree_wait(1)
+
+            @pl.when(floor)
+            def _():
+                tree(2, "start")
+
+    finish1 = gather(CHILD_PANELS, False, (), first_rows, loct, u1, w1, None, sems[0:12], couple_child)
+
+    @pl.when(jnp.logical_not(floor))
+    def _():
+        tree_wait(2)
+
+    @pl.when(line)
+    def _():
+        tree(1, "wait")
+
+    @pl.when(floor)
+    def _():
+        tree(2, "wait")
 
     for c in range(2):
-        l10 = dot(pp1[c].reshape(B, B), ginv_ref[c, 0])
+        l10 = dot(pp1[c], ginv_ref[c, 0])
         lt[c] = rhs3(l10.T)
         v0 = u1[c]
         v1 = u1[2 + c] - dot(l10, v0)
@@ -304,82 +403,117 @@
     def x_device(dx):
         return (f, y, 4 * ring(x, dx) + z)
 
-    def first(s, dz, dx):
-        sem = (h1s.at[s, dz, dx], h1r.at[s, dz, dx])
-        src = stg.at[s, dz, dx]
-        if dz and (s == 0 or not dx):
-            dst = hop.at[s, dz, dx] if dx else fin.at[s, dx, dz]
-            return remote(src, dst, *sem, z_device(dz))
-        dst = hop.at[s, dz, dx] if dz else fin.at[s, dx, dz]
+    def first(s, h, dz, dx):
+        sem = (h1s.at[s, h, dz, dx], h1r.at[s, h, dz, dx])
+        rows = pl.ds(h * HALF, HALF)
+        src = stg.at[s, dz, dx, rows]
+        if not dx:
+            return remote(src, fin.at[s, dx, dz, rows], *sem, z_device(dz))
+        dst = hop.at[s, dz, dx, rows] if dz else fin.at[s, dx, dz, rows]
         return remote(src, dst, *sem, x_device(dx))
 
-    def second(s, dz, dx):
-        sem = (h2s.at[s, dz, dx], h2r.at[s, dz, dx])
-        device = x_device(dx) if s == 0 else z_device(dz)
-        return remote(hop.at[s, dz, dx], fin.at[s, dx, dz], *sem, device)
-
-    def begin(s, dz, dx):
-        if not (dz or dx):
-            fin[s, 0, 0] = slab(0, s, 0)
-            return
-        stg[s, dz, dx] = slab(dz, s, dx)
-        first(s, dz, dx).start()
-
-    order = [(0, 0, 0)] + [(0, dz, 0) for dz in AROUND]
-    for d in AROUND:
-        order += [(1, d, dx) for dx in AROUND]
-        order += [(0, dz, d) for dz in AROUND]
-    order += [(1, 0, 0)]
-    for d in AROUND:
-        order += [(1, 0, d), (0, 0, d), (1, d, 0)]
-    for item in order:
-        begin(*item)
-
-    def pass_y(s, dx):
+    def second(s, h, dz, dx):
+        sem = (h2s.at[s, h, dz, dx], h2r.at[s, h, dz, dx])
+        rows = pl.ds(h * HALF, HALF)
+        return remote(hop.at[s, dz, dx, rows], fin.at[s, dx, dz, rows], *sem, z_device(dz))
+
+    def compute(s, items):
+        for dz, dx in items:
+            if dz or dx:
+                stg[s, dz, dx] = slab(dz, s, dx)
+            else:
+                fin[s, 0, 0] = slab(0, s, 0)
+
+    def start(s, h, items):
+        for dz, dx in items:
+            first(s, h, dz, dx).start()
+
+    own = [(0, 0)]
+    straight = [(dz, 0) for dz in AROUND]
+    rounds = [[(dz, dx) for dx in AROUND] for dz in (1, 3, 2, 0)]
+
+    def forward(s, h, dx):
+        for dz in AROUND:
+            first(s, h, dz, dx).wait_recv()
+            second(s, h, dz, dx).start()
+
+    def y_copy(dy, s, h, dx):
+        rows = pl.ds(h * HALF, HALF)
+        sem = (ys.at[dy, s, h, dx], yr.at[dy, s, h, dx])
+        return remote(sy.at[dy, s, dx, :, rows], got.at[dy, s, dx, :, rows], *sem, (f, ring(y, dy), 4 * x + z))
+
+    home = ring(z, -y)
+    child_of = [(slot_of(home, s) >= 3) for s in range(2)]
+
+    def pass_y(s, h, dx):
         for dz in range(4):
             if dz and dx:
-                second(s, dz, dx).wait_recv()
+                second(s, h, dz, dx).wait_recv()
             elif dz or dx:
-                first(s, dz, dx).wait_recv()
-        slot = slot_of(ring(z, -y), s)
+                first(s, h, dz, dx).wait_recv()
+        rows = slice(h * HALF, (h + 1) * HALF)
         for dy in (1, 3, 2, 0):
             for t in range(3):
-                res = jnp.where(slot >= 3, residues[3 + t], residues[t])
+                res = jnp.where(child_of[s], residues[3 + t], residues[t])
                 dz = lax.rem(z - ring(y, dy) + res + 8, 4)
-                block = pick([fin[s, dx, k, :, t * B : (t + 1) * B] for k in range(4)], dz)
+                block = pick([fin[s, dx, k, rows, t * B : (t + 1) * B] for k in range(4)], dz)
                 if dy:
-                    sy[dy, s, dx, t] = block
+                    sy[dy, s, dx, t, rows, :] = block
                 else:
-                    got[0, s, dx, t] = block
+                    got[0, s, dx, t, rows, :] = block
             if dy:
-                y_copy(dy, s, dx).start()
-
-    def y_copy(dy, s, dx):
-        return remote(
-            sy.at[dy, s, dx], got.at[dy, s, dx], ys.at[dy, s, dx], yr.at[dy, s, dx], (f, ring(y, dy), 4 * x + z)
-        )
-
-    def forward(s, d):
-        for e in AROUND:
-            dz, dx = (e, d) if s == 0 else (d, e)
-            first(s, dz, dx).wait_recv()
-            second(s, dz, dx).start()
-
-    forward(1, 1)
-    pass_y(0, 0)
-    forward(0, 1)
-    forward(1, 3)
-    forward(0, 3)
-    forward(1, 2)
-    forward(0, 2)
-    pass_y(1, 0)
-    for dx in AROUND:
-        pass_y(0, dx)
-        pass_y(1, dx)
-    for s in range(2):
+                y_copy(dy, s, h, dx).start()
+
+    compute(0, straight)
+    start(0, 0, straight)
+    for items in rounds:
+        compute(0, items)
+        start(0, 0, items)
+    compute(0, own)
+    start(0, 1, straight)
+    for items in rounds:
+        start(0, 1, items)
+    pass_y(0, 0, 0)
+    compute(1, straight + own)
+    start(1, 0, straight)
+    pass_y(0, 1, 0)
+    forward(0, 0, 1)
+    compute(1, rounds[0])
+    start(1, 0, rounds[0])
+    forward(0, 0, 3)
+    compute(1, rounds[1])
+    start(1, 0, rounds[1])
+    pass_y(0, 0, 1)
+    forward(0, 0, 2)
+    compute(1, rounds[2])
+    start(1, 0, rounds[2])
+    pass_y(0, 0, 3)
+    compute(1, rounds[3])
+    start(1, 0, rounds[3])
+    start(1, 1, straight)
+    for items in rounds:
+        start(1, 1, items)
+    pass_y(1, 0, 0)
+    pass_y(0, 0, 2)
+    forward(0, 1, 1)
+    forward(0, 1, 3)
+    pass_y(0, 1, 1)
+    forward(0, 1, 2)
+    pass_y(0, 1, 3)
+    pass_y(1, 1, 0)
+    pass_y(0, 1, 2)
+    for h in range(2):
+        forward(1, h, 1)
+        forward(1, h, 3)
+        pass_y(1, h, 1)
+        forward(1, h, 2)
+        pass_y(1, h, 3)
+        pass_y(1, h, 2)
+    halves = [(s, h) for s in range(2) for h in range(2)]
+    for s, h in halves:
         for dx in range(4):
             for dy in AROUND:
-                y_copy(dy, s, dx).wait_recv()
+                y_copy(dy, s, h, dx).wait_recv()
 
     loads[2].wait()
 
@@ -419,25 +553,30 @@
         for t in range(3):
             loct[2 + i, t] = turned(acc[i, :, t * B : (t + 1) * B])
 
+    store = pltpu.make_async_copy(acc, a_ref, load_sem.at[0])
     bounds = [(2, 5), (5, 8), (8, 24)]
+
+    def add_rest(n):
+        add_rows(*bounds[n])
+        if n == 2:
+            store.start()
+
     finish2 = gather(
         PARENT_PANELS, True, PARENT_COUPLINGS, acc, loct.at[2:4], u2, w2, pp2, sems[12:24],
-        lambda n: add_rows(*bounds[n]),
+        add_rest,
     )
-    store = pltpu.make_async_copy(acc, a_ref, load_sem.at[0])
-    store.start()
     finish1()
     finish2()
-    for s in range(2):
+    for s, h in halves:
         for dz in range(4):
             for dx in range(4):
                 if dz or dx:
-                    first(s, dz, dx).wait_send()
+                    first(s, h, dz, dx).wait_send()
                 if dz and dx:
-                    second(s, dz, dx).wait_send()
+                    second(s, h, dz, dx).wait_send()
         for dx in range(4):
             for dy in AROUND:
-                y_copy(dy, s, dx).wait_send()
+                y_copy(dy, s, h, dx).wait_send()
     store.wait()
 
 
@@ -459,7 +598,7 @@
             pltpu.VMEM((4, 3) + TILE, F32),
             pltpu.VMEM((4,) + slab, F32),
             pltpu.VMEM((1, 4, 4, 3) + TILE, F32),
-            pltpu.VMEM((2,) + TILE, F32),
+            pltpu.VMEM((2, B, B), F32),
             pltpu.VMEM((2, 3 * B, B), BF16),
             pltpu.VMEM((2, 6 * B, 3 * B), BF16),
             pltpu.VMEM((2, 4, 4) + slab, F32),
@@ -468,12 +607,14 @@
             pltpu.VMEM((4, 2, 4, 3, B, B), F32),
             pltpu.VMEM((4, 2, 4, 3, B, B), F32),
             DMA((3,)),
-            DMA((2, 4, 4)),
-            DMA((2, 4, 4)),
-            DMA((2, 4, 4)),
-            DMA((2, 4, 4)),
-            DMA((4, 2, 4)),
-            DMA((4, 2, 4)),
+            DMA((3, 4)),
+            DMA((3,)),
+            DMA((2, 2, 4, 4)),
+            DMA((2, 2, 4, 4)),
+            DMA((2, 2, 4, 4)),
+            DMA((2, 2, 4, 4)),
+            DMA((4, 2, 2, 4)),
+            DMA((4, 2, 2, 4)),
         ]
         + gather_sems(4, 1)
         + gather_sems(5, 4),
@@ -484,7 +625,7 @@
     )(block_map, children.reshape((2, 12) + slab), parent.reshape((24,) + slab), inverses)
 
 
-def parent_kernel(a_ref, u_ref, w_ref, pp_ref, g_ref, out_ref, cur, ltc, v_ref, q_ref, qcat, gcat, wt):
+def parent_kernel(a_ref, u_ref, w_ref, pp_ref, g_ref, out_ref, panel, lth, ltl, q_ref, qcat, gcat, wh, wl):
     f, y, x, z = place()
     steps = range(5)
     col = 4 * x + z
@@ -492,29 +633,46 @@
 
     @pl.when(n == 0)
     def _():
-        for k in range(10):
-            cur[k] = pp_ref[k].reshape(B, B)
-        for j in steps:
-            v_ref[j] = u_ref[j]
+        for k in steps:
+            for j in range(k):
+                block = pp_ref[PAIR[k, j]].reshape(B, B)
+                panel[k * B : (k + 1) * B, j * B : (j + 1) * B] = block
+                panel[j * B : (j + 1) * B, k * B : (k + 1) * B] = block.T
+            panel[k * B : (k + 1) * B, k * B : (k + 1) * B] = jnp.zeros((B, B), F32)
+            panel[k * B : (k + 1) * B, 5 * B :] = u_ref[k]
+            gcat[k] = rhs3(g_ref[k])
         for j in range(4):
-            for k in range(j + 1, 5):
-                l_kj = dot(cur[PAIR[k, j]], g_ref[j])
-                ltc[PAIR[k, j]] = l_kj.T
-                for i in range(j + 1, k):
-                    cur[PAIR[k, i]] -= dot(l_kj, cur[PAIR[i, j]].T)
-                v_ref[k] -= dot(l_kj, v_ref[j])
+            here, later = slice(j * B, (j + 1) * B), slice((j + 1) * B, 5 * B)
+            low = mul3(lhs3(panel[later, here]), gcat[j])
+            high, rest = split(low.T)
+            lth[here, later] = high
+            ltl[here, later] = rest
+            panel[later, (j + 1) * B :] -= dot(low, panel[here, (j + 1) * B :])
         for k in steps:
-            q_ref[k * B : (k + 1) * B, :] = dot(g_ref[k], v_ref[k])
-            gcat[k] = rhs3(g_ref[k])
+            q_ref[k * B : (k + 1) * B, :] = dot(g_ref[k], panel[k * B : (k + 1) * B, 5 * B :])
         qcat[...] = rhs3(q_ref[...])
 
-    for k in steps:
-        w = w_ref[0, k, :, 0].reshape(4 * B, B)
-        if k:
-            low = jnp.concatenate([ltc[PAIR[k, j]] for j in range(k)], axis=0)
-            w = w - dot(wt[:, 0 : k * B], low)
-        wt[:, k * B : (k + 1) * B] = w
-    out = a_ref[...].reshape(4 * B, 3 * B) - mul3(lhs3(wt[...]), qcat[...])
+    def keep(k, w):
+        high, rest = split(w)
+        wh[:, k * B : (k + 1) * B] = high
+        wl[:, k * B : (k + 1) * B] = rest
+
+    def left(low, high):
+        return jnp.concatenate([wh[:, low:high], wh[:, low:high], wl[:, low:high]], axis=1)
+
+    def earlier(k0, k1, j0, j1):
+        rows, cols = slice(j0 * B, j1 * B), slice(k0 * B, k1 * B)
+        low = jnp.concatenate([lth[rows, cols], ltl[rows, cols], lth[rows, cols]], axis=0)
+        return mul3(left(j0 * B, j1 * B), low)
+
+    raw = [w_ref[0, k, :, 0].reshape(4 * B, B) for k in steps]
+    keep(0, raw[0])
+    keep(1, raw[1] - earlier(1, 2, 0, 1))
+    pair = jnp.concatenate([raw[2], raw[3]], axis=1) - earlier(2, 4, 0, 2)
+    keep(2, pair[:, 0:B])
+    keep(3, pair[:, B:] - earlier(3, 4, 2, 3))
+    keep(4, raw[4] - earlier(4, 5, 0, 4))
+    out = a_ref[...].reshape(4 * B, 3 * B) - mul3(left(0, 5 * B), qcat[...])
     out_ref[...] = out.reshape(4, B, 3 * B)
 
     @pl.when((f == 0) & (col < 5))
@@ -523,7 +681,7 @@
 
             @pl.when(col == k)
             def _():
-                scaled = mul3(lhs3(wt[:, k * B : (k + 1) * B]), gcat[k])
+                scaled = mul3(left(k * B, (k + 1) * B), gcat[k])
                 for i in range(4):
                     slot = 4 * n + i
                     row = 4 * slot + y
@@ -534,7 +692,7 @@
 
                     @pl.when(row == k)
                     def _():
-                        out_ref[i, :, 0:B] = v_ref[k, :, 0:B]
+                        out_ref[i, :, 0:B] = panel[k * B : (k + 1) * B, 5 * B : 6 * B]
 
     @pl.when(n == 0)
     def _():
@@ -542,10 +700,10 @@
 
             @pl.when(y == k % 4)
             def _():
-                panel = q_ref[k * B : (k + 1) * B, :]
-                keep = (f == 0) & (col <= k)
-                out_ref[k // 4, :, B:] = panel[:, B:]
-                out_ref[k // 4, :, 0:B] = jnp.where(keep, out_ref[k // 4, :, 0:B], panel[:, 0:B])
+                rows = q_ref[k * B : (k + 1) * B, :]
+                done = (f == 0) & (col <= k)
+                out_ref[k // 4, :, B:] = rows[:, B:]
+                out_ref[k // 4, :, 0:B] = jnp.where(done, out_ref[k // 4, :, 0:B], rows[:, 0:B])
 
 
 def parent_update(a, u, w, pp, inverses):
@@ -565,13 +723,14 @@
         ],
         out_specs=pl.BlockSpec((4, B, 3 * B), lambda n: (n, 0, 0)),
         scratch_shapes=[
-            pltpu.VMEM((10, B, B), F32),
-            pltpu.VMEM((10, B, B), F32),
-            pltpu.VMEM((5, B, 3 * B), F32),
+            pltpu.VMEM((5 * B, 8 * B), F32),
+            pltpu.VMEM((5 * B, 5 * B), BF16),
+            pltpu.VMEM((5 * B, 5 * B), BF16),
             pltpu.VMEM((5 * B, 3 * B), F32),
             pltpu.VMEM((15 * B, 3 * B), BF16),
             pltpu.VMEM((5, 3 * B, B), BF16),
-            pltpu.VMEM((4 * B, 5 * B), F32),
+            pltpu.VMEM((4 * B, 5 * B), BF16),
+            pltpu.VMEM((4 * B, 5 * B), BF16),
         ],
         compiler_params=pltpu.CompilerParams(vmem_limit_bytes=48 << 20),
         name="parent_update",

time: 253 us -> 220 us (0.87)
  the two profiles are of different devices: /device:TPU:1 before, /device:TPU:31 now
where the time goes in v3:
time: 220 us
  Pallas kernels  217 us (99%)
  local copies, waits for them, and re-layouts  2.29 us (1%)
    pallas_call x1, Pallas kernels, assemble(): pl.pallas_call(assemble_kernel, out_shape=(jax.ShapeDtypeStruct((24,) + s...  195 us
    pallas_call x1, Pallas kernels, parent_update(): pl.pallas_call(parent_kernel, out_shape=jax.ShapeDtypeStruct((24, B, 3 *...  21.9 us

profile of v3, /device:TPU:31, one launch (start us, length us, event | category | flops | bytes accessed | tf_op | source)
XLA Modules:
  0.0 219.7 jit_solution(13290919981863778108)
XLA Ops:
  0.0 0.0 copy-start.2
  0.0 195.4 %assemble.1 = (f32[24,128,384]{2,1,0:T(8,128)}, f32[5,128,384]{2,1,0:T(8,128)}, f32[2,5,4,3,4,2,16,128]{7,6,5,4,3,2,1,0:T(8,128)}, f32[10,4,2,16,128]{4,3,2,1,0:T(8,128)}) custom-call(s32[2,48]{1,0:T(2,128)} %map_ref.1, f32[2,12,128,384]{3,2,1,0:T(8,128)} %bitcast.3, f32[24,128,384]{2,1,0:T(8,128)} %bitcast.4, f32[2,2,128,128]{3,2,1,0:T(8,128)} %ginv_ref.1), custom_call_target="tpu_custom_call" | custom-call | tf_op jit(solution)/shard_map/assemble/pallas_call | solution.py:585
  195.4 0.0 copy-done.2
  195.4 0.0 copy-start
  195.5 1.2 copy-done
  196.6 0.0 copy-start.1
  196.6 1.1 copy-done.1
  197.7 21.9 %parent_update.1 = f32[24,128,384]{2,1,0:T(8,128)} custom-call(f32[24,128,384]{2,1,0:T(8,128)} %get-tuple-element.9.a_ref, f32[5,128,384]{2,1,0:T(8,128)S(1)} %copy-done, f32[2,5,4,3,4,2,16,128]{7,6,5,4,3,2,1,0:T(8,128)} %get-tuple-element.11.w_ref, f32[10,4,2,16,128]{4,3,2,1,0:T(8,128)S(1)} %copy-done.1, f32[5,128,128]{2,1,0:T(8,128)S(1)} %copy-done.2), custom_call_target="tpu_custom_call" | custom-call | tf_op jit(solution)/shard_map/parent_update/pallas_call | solution.py:713
Async XLA Ops:
  0.0 195.4 %copy-start.2 = (f32[5,128,128]{2,1,0:T(8,128)S(1)}, f32[5,128,128]{2,1,0:T(8,128)}, u32[]{:S(2)}) copy-start(f32[5,128,128]{2,1,0:T(8,128)} %g_ref.1) | copy-start | bytes 983044
  195.4 1.2 copy-start
  196.6 1.1 copy-start.1

commit v4 on v3

--- a/solution.py
+++ b/solution.py
@@ -64,178 +64,190 @@
     return out
 
 
-def gather(panels, cross, couplings, loc, loct, u_ref, w_ref, pp_ref, sems, idle):
+def gather(panels, own, active, cross, couplings, loc, loct, u_ref, w_ref, pp_ref, sems):
     su, ru, ss, rs, s2, r2, s3, r3, s4, r4, s5, r5 = sems
     f, y, x, z = place()
-    own = f if cross else 0
     parts = (slice(0, 1), slice(1, 3)) if cross else (slice(0, 3),)
+    here, other = (f, y, 4 * x + z), (1 - f, y, 4 * x + z)
     late = []
+
+    def stage(write):
+        write() if active is None else pl.when(active)(write)
+
+    def each(step, op):
+        for p, (sy, i) in enumerate(panels):
+            pl.when(y == sy)(functools.partial(step, p, op))
 
     def scatter(p, op):
         i = panels[p][1]
         for zz in range(4):
             mine = (y == z) & (z == zz)
-            src, dst = loct.at[i, :, zz], w_ref.at[own, p, x, :, zz]
+            src, dst = loct(i).at[:, zz], w_ref.at[own, p, x, :, zz]
             cp = remote(src, dst, ss.at[p, zz], rs.at[p], (f, z, 4 * x + zz))
-            here = pltpu.make_async_copy(src, dst, ss.at[p, zz])
 
             @pl.when(jnp.logical_not(mine))
             def _():
                 cp.start() if op == "start" else cp.wait_send()
 
-            @pl.when(mine)
+            if op == "start":
+                pl.when(mine)(pltpu.make_async_copy(src, dst, ss.at[p, zz]).start)
+
+    def column(p, op):
+        src = loc(panels[p][1])
+        for dy in AROUND:
+            cp = remote(src, u_ref.at[p], su.at[p, dy], ru.at[p], (f, ring(y, dy), 4 * x + z))
+            cp.start() if op == "start" else cp.wait_send()
+        local = pltpu.make_async_copy(src, u_ref.at[p], su.at[p, 0])
+        local.start() if op == "start" else local.wait()
+
+    def arrived(region, rsem):
+        remote(region, region, s2.at[0, 0], rsem, here).wait_recv()
+
+    def pieces():
+        for p, (sy, i) in enumerate(panels):
+            region = w_ref.at[own, p, x, :, z]
+
+            @pl.when(jnp.logical_not((y == sy) & (y == z)))
             def _():
-                here.start() if op == "start" else here.wait()
-
-    def column(p, op):
-        i = panels[p][1]
-        for dy in AROUND:
-            cp = remote(loc.at[i], u_ref.at[p], su.at[p, dy], ru.at[p], (f, ring(y, dy), 4 * x + z))
-            cp.start() if op == "start" else cp.wait_send()
-        here = pltpu.make_async_copy(loc.at[i], u_ref.at[p], su.at[p, 0])
-        here.start() if op == "start" else here.wait()
-
-    for p, (sy, i) in enumerate(panels):
-        pl.when(y == sy)(functools.partial(scatter, p, "start"))
-    idle(0)
-    for p, (sy, i) in enumerate(panels):
-        region = w_ref.at[own, p, x, :, z]
-
-        @pl.when(jnp.logical_not((y == sy) & (y == z)))
-        def _():
-            remote(region, region, ss.at[p, 0], rs.at[p], (f, y, 4 * x + z)).wait_recv()
-
-        @pl.when((y == sy) & (y == z))
-        def _():
-            for zz in range(4):
-
-                @pl.when(z == zz)
-                def _():
-                    pltpu.make_async_copy(region, region, ss.at[p, zz]).wait()
-
-    along_x = [w_ref.at[own, :, ring(x, -d), :, z, 0] for d in range(4)]
-    along_z = [w_ref.at[own, :, x, :, ring(z, -d), 1] for d in range(4)]
-
-    def part_x(d, ts, front=own):
-        return w_ref.at[front, :, :, ts, ring(z, -d), 0]
-
-    def part_z(d, ts, front=own):
-        return w_ref.at[front, :, ring(x, -d), ts, :, 1]
-
-    def send(*args):
-        cp = remote(*args)
-        cp.start()
-        late.append(cp)
-
-    def arrived(region, rsem):
-        remote(region, region, s2.at[0, 0], rsem, (f, y, 4 * x + z)).wait_recv()
+                arrived(region, rs.at[p])
+
+            @pl.when((y == sy) & (y == z))
+            def _():
+                for zz in range(4):
+
+                    @pl.when(z == zz)
+                    def _():
+                        pltpu.make_async_copy(region, region, ss.at[p, zz]).wait()
+
+    def along_x(d):
+        return w_ref.at[own, :, ring(x, -d), :, z, 0]
+
+    def along_z(d):
+        return w_ref.at[own, :, x, :, ring(z, -d), 1]
+
+    def part_x(d, ts):
+        return w_ref.at[own, :, :, ts, ring(z, -d), 0]
+
+    def part_z(d, ts):
+        return w_ref.at[own, :, ring(x, -d), ts, :, 1]
+
+    def send(build):
+        late.append(build)
+        remote(*build()).start()
 
     def across(q, n, region):
         if cross:
-            send(region, region, s4.at[q, n], r4.at[q, n], (1 - f, y, 4 * x + z))
-
-    for d in AROUND:
-        send(along_x[0], along_x[0], s2.at[0, d], r2.at[0, d], (f, y, 4 * ring(x, d) + z))
-        send(along_z[0], along_z[0], s2.at[1, d], r2.at[1, d], (f, y, 4 * x + ring(z, d)))
-    for p, (sy, i) in enumerate(panels):
-        pl.when(y == sy)(functools.partial(column, p, "start"))
-    idle(1)
-    for d in AROUND:
-        arrived(along_x[d], r2.at[0, d])
-    for q, ts in enumerate(parts):
+            send(lambda: (region(), region(), s4.at[q, n], r4.at[q, n], other))
+
+    def second_x():
         for d in AROUND:
-            region = part_x(0, ts)
-            send(region, region, s3.at[0, q, d], r3.at[0, q, d], (f, y, 4 * x + ring(z, d)))
-    for d in AROUND:
-        arrived(along_z[d], r2.at[1, d])
-    for q, ts in enumerate(parts):
+            send(lambda d=d: (along_x(0), along_x(0), s2.at[0, d], r2.at[0, d], (f, y, 4 * ring(x, d) + z)))
+            send(lambda d=d: (along_z(0), along_z(0), s2.at[1, d], r2.at[1, d], (f, y, 4 * x + ring(z, d))))
+
+    def third_z():
         for d in AROUND:
-            region = part_z(0, ts)
-            send(region, region, s3.at[1, q, d], r3.at[1, q, d], (f, y, 4 * ring(x, d) + z))
-    for q, ts in enumerate(parts):
-        across(q, 0, part_x(0, ts))
-        across(q, 4, part_z(0, ts))
-    idle(2)
+            arrived(along_x(d), r2.at[0, d])
+        for q, ts in enumerate(parts):
+            for d in AROUND:
+
+                def build(q=q, ts=ts, d=d):
+                    region = part_x(0, ts)
+                    return region, region, s3.at[0, q, d], r3.at[0, q, d], (f, y, 4 * x + ring(z, d))
+
+                send(build)
+
+    def third_x():
+        for d in AROUND:
+            arrived(along_z(d), r2.at[1, d])
+        for q, ts in enumerate(parts):
+            for d in AROUND:
+
+                def build(q=q, ts=ts, d=d):
+                    region = part_z(0, ts)
+                    return region, region, s3.at[1, q, d], r3.at[1, q, d], (f, y, 4 * ring(x, d) + z)
+
+                send(build)
+        for q, ts in enumerate(parts):
+            across(q, 0, functools.partial(part_x, 0, ts))
+            across(q, 4, functools.partial(part_z, 0, ts))
 
     def collect(q, ts):
         for d in AROUND:
             arrived(part_x(d, ts), r3.at[0, q, d])
-            across(q, d, part_x(d, ts))
+            across(q, d, functools.partial(part_x, d, ts))
             arrived(part_z(d, ts), r3.at[1, q, d])
-            across(q, 4 + d, part_z(d, ts))
-
-    collect(0, parts[0])
-    if cross:
-
-        def couple(e, op):
-            sy, base, n, m = couplings[e]
-            src, dst = w_ref.at[0, 0:n, m, 0], pp_ref.at[base : base + n]
-            for dy in AROUND:
-                cp = remote(src, dst, s5.at[e, dy], r5.at[e], (f, ring(y, dy), 4 * x + z))
-                cp.start() if op == "start" else cp.wait_send()
-            here = pltpu.make_async_copy(src, dst, s5.at[e, 0])
-            here.start() if op == "start" else here.wait()
-
-        pair = remote(pp_ref, pp_ref, s4.at[0, 8], r4.at[0, 8], (1 - f, y, 4 * x + z))
-
-        @pl.when(f == 0)
-        def _():
-            for e, (sy, base, n, m) in enumerate(couplings):
-                pl.when(y == sy)(functools.partial(couple, e, "start"))
-
-    for q in range(1, len(parts)):
-        collect(q, parts[q])
-    if cross:
-
-        @pl.when(f == 0)
-        def _():
-            for e, (sy, base, n, m) in enumerate(couplings):
-
-                @pl.when(y != sy)
-                def _():
-                    arrived(pp_ref.at[base : base + n], r5.at[e])
-
-                pl.when(y == sy)(functools.partial(couple, e, "wait"))
-            pair.start()
-
-    for p, (sy, i) in enumerate(panels):
-
-        @pl.when(y != sy)
-        def _():
-            arrived(u_ref.at[p], ru.at[p])
-
-    if cross:
+            across(q, 4 + d, functools.partial(part_z, d, ts))
+
+    def couple(e, op):
+        sy, base, n, m = couplings[e]
+        src, dst = w_ref.at[0, 0:n, m, 0], pp_ref.at[base : base + n]
+        for dy in AROUND:
+            cp = remote(src, dst, s5.at[e, dy], r5.at[e], (f, ring(y, dy), 4 * x + z))
+            cp.start() if op == "start" else cp.wait_send()
+        local = pltpu.make_async_copy(src, dst, s5.at[e, 0])
+        local.start() if op == "start" else local.wait()
+
+    def pair():
+        return remote(pp_ref, pp_ref, s4.at[0, 8], r4.at[0, 8], other)
+
+    def fourth():
+        collect(0, parts[0])
+        for e, (sy, base, n, m) in enumerate(couplings):
+            pl.when(y == sy)(functools.partial(couple, e, "start"))
+        for q in range(1, len(parts)):
+            collect(q, parts[q])
+        for e, (sy, base, n, m) in enumerate(couplings):
+
+            @pl.when(y != sy)
+            def _():
+                arrived(pp_ref.at[base : base + n], r5.at[e])
+
+            pl.when(y == sy)(functools.partial(couple, e, "wait"))
+        if couplings:
+            pair().start()
+        for p, (sy, i) in enumerate(panels):
+
+            @pl.when(y != sy)
+            def _():
+                arrived(u_ref.at[p], ru.at[p])
+
+        each(column, "wait")
+
+    def handed():
         for q, ts in enumerate(parts):
             for d in range(4):
-                arrived(part_x(d, ts, 1 - f), r4.at[q, d])
-                arrived(part_z(d, ts, 1 - f), r4.at[q, 4 + d])
-
-        @pl.when(f == 0)
-        def _():
-            pair.wait_send()
-
-        @pl.when(f == 1)
-        def _():
-            pair.wait_recv()
+                arrived(part_x(d, ts), r4.at[q, d])
+                arrived(part_z(d, ts), r4.at[q, 4 + d])
+        if couplings:
+            pair().wait_recv()
 
     def finish():
-        def scatter_rest(p):
-            i = panels[p][1]
-            for zz in range(4):
-
-                @pl.when(jnp.logical_not((y == z) & (z == zz)))
-                def _():
-                    src, dst = loct.at[i, :, zz], w_ref.at[own, p, x, :, zz]
-                    remote(src, dst, ss.at[p, zz], rs.at[p], (f, z, 4 * x + zz)).wait_send()
-
-        for p, (sy, i) in enumerate(panels):
-            pl.when(y == sy)(functools.partial(scatter_rest, p))
-        for cp in late:
-            cp.wait_send()
-
-    for p, (sy, i) in enumerate(panels):
-        pl.when(y == sy)(functools.partial(column, p, "wait"))
-    return finish
+        each(scatter, "wait")
+        for build in late:
+            remote(*build()).wait_send()
+        if couplings:
+            pair().wait_send()
+
+    stage(lambda: each(scatter, "start"))
+    yield
+
+    @stage
+    def _():
+        pieces()
+        second_x()
+        each(column, "start")
+
+    yield
+    stage(third_z)
+    yield
+    stage(third_x)
+    yield
+    stage(fourth)
+    yield
+    if cross:
+        pl.when(jnp.logical_not(active))(handed)
+    stage(finish)
+    yield
 
 
 def gather_sems(count, couplings):
@@ -271,10 +283,11 @@
     loads = [
         pltpu.make_async_copy(child_ref.at[:, 0:1], fr.at[:, 0:1], load_sem.at[0]),
         pltpu.make_async_copy(child_ref.at[:, 1:12], fr.at[:, 1:12], load_sem.at[1]),
-        pltpu.make_async_copy(parent_ref, acc, load_sem.at[2]),
+        pltpu.make_async_copy(parent_ref.at[0:2], acc.at[0:2], load_sem.at[2]),
+        pltpu.make_async_copy(parent_ref.at[2:24], acc.at[2:24], load_sem.at[3]),
     ]
-    for cp in loads:
-        cp.start()
+    for n in (0, 2, 1, 3):
+        loads[n].start()
 
     barrier = pltpu.get_barrier_semaphore()
     greeted = []
@@ -312,7 +325,6 @@
             loct[c, t] = turned(fr[c, 0, :, t * B : (t + 1) * B])
     pl.semaphore_wait(barrier, len(greeted))
 
-    first_rows = fr.at[:, 0]
 
     def tree_y(op):
         src = fr.at[:, 0, :, 0:B]
@@ -333,38 +345,55 @@
 
     root, line, floor = (y == 1) & (x == 0) & (z == 0), (x == 0) & (z == 0), z == 0
 
-    def couple_child(n):
-        if n == 0:
-
-            @pl.when(root)
-            def _():
-                tree_y("start")
-
-        if n == 1:
-
-            @pl.when(root)
-            def _():
-                tree_y("wait")
-
-            @pl.when(line & jnp.logical_not(root))
-            def _():
-                tree_wait(0)
-
-            @pl.when(line)
-            def _():
-                tree(1, "start")
-
-        if n == 2:
-
-            @pl.when(floor & jnp.logical_not(line))
-            def _():
-                tree_wait(1)
-
-            @pl.when(floor)
-            def _():
-                tree(2, "start")
-
-    finish1 = gather(CHILD_PANELS, False, (), first_rows, loct, u1, w1, None, sems[0:12], couple_child)
+    panel1 = gather(CHILD_PANELS, 0, None, False, (), lambda i: fr.at[i, 0], lambda i: loct.at[i], u1, w1, None, sems[0:12])
+    panel2a = gather(
+        PARENT_PANELS, 1, f == 1, True, (), lambda i: acc.at[i], lambda i: loct.at[2 + i], u2, w2, pp2, sems[12:24]
+    )
+    panel2b = gather(
+        PARENT_PANELS, 0, f == 0, True, PARENT_COUPLINGS, lambda i: acc.at[i], lambda i: loct.at[4 + i], u2, w2, pp2,
+        sems[24:36],
+    )
+    next(panel1)
+
+    @pl.when(root)
+    def _():
+        tree_y("start")
+
+    loads[2].wait()
+
+    @pl.when(f == 1)
+    def _():
+        for i in range(2):
+            for t in range(3):
+                loct[2 + i, t] = turned(acc[i, :, t * B : (t + 1) * B])
+
+    next(panel2a)
+    next(panel1)
+
+    @pl.when(root)
+    def _():
+        tree_y("wait")
+
+    @pl.when(line & jnp.logical_not(root))
+    def _():
+        tree_wait(0)
+
+    @pl.when(line)
+    def _():
+        tree(1, "start")
+
+    next(panel1)
+    next(panel1)
+
+    @pl.when(floor & jnp.logical_not(line))
+    def _():
+        tree_wait(1)
+
+    @pl.when(floor)
+    def _():
+        tree(2, "start")
+
+    next(panel1)
 
     @pl.when(jnp.logical_not(floor))
     def _():
@@ -478,6 +507,7 @@
     start(1, 0, straight)
     pass_y(0, 1, 0)
     forward(0, 0, 1)
+    next(panel2a)
     compute(1, rounds[0])
     start(1, 0, rounds[0])
     forward(0, 0, 3)
@@ -507,6 +537,9 @@
         forward(1, h, 3)
         pass_y(1, h, 1)
         forward(1, h, 2)
+        if h:
+            next(panel2a)
+            next(panel2a)
         pass_y(1, h, 3)
         pass_y(1, h, 2)
     halves = [(s, h) for s in range(2) for h in range(2)]
@@ -515,7 +548,7 @@
             for dy in AROUND:
                 y_copy(dy, s, h, dx).wait_recv()
 
-    loads[2].wait()
+    loads[3].wait()
 
     def landing(c, target):
         block, found = jnp.int32(0), jnp.bool_(False)
@@ -548,25 +581,33 @@
 
         lax.fori_loop(low, high, step, 0)
 
-    add_rows(0, 2)
-    for i in range(2):
-        for t in range(3):
-            loct[2 + i, t] = turned(acc[i, :, t * B : (t + 1) * B])
+    @pl.when(f == 0)
+    def _():
+        add_rows(0, 2)
+        for i in range(2):
+            for t in range(3):
+                loct[4 + i, t] = turned(acc[i, :, t * B : (t + 1) * B])
 
     store = pltpu.make_async_copy(acc, a_ref, load_sem.at[0])
-    bounds = [(2, 5), (5, 8), (8, 24)]
-
-    def add_rest(n):
-        add_rows(*bounds[n])
-        if n == 2:
-            store.start()
-
-    finish2 = gather(
-        PARENT_PANELS, True, PARENT_COUPLINGS, acc, loct.at[2:4], u2, w2, pp2, sems[12:24],
-        add_rest,
-    )
-    finish1()
-    finish2()
+    next(panel2b)
+
+    add_rows(2, 5)
+    next(panel2b)
+    next(panel2a)
+
+    @pl.when(f == 1)
+    def _():
+        add_rows(0, 2)
+
+    add_rows(5, 8)
+    next(panel2b)
+    next(panel2b)
+    add_rows(8, 24)
+    store.start()
+    next(panel2b)
+    next(panel2a)
+    next(panel2b)
+    next(panel1)
     for s, h in halves:
         for dz in range(4):
             for dx in range(4):
@@ -595,7 +636,7 @@
         scratch_shapes=[
             pltpu.VMEM((2, 12) + slab, F32),
             pltpu.VMEM((24,) + slab, F32),
-            pltpu.VMEM((4, 3) + TILE, F32),
+            pltpu.VMEM((6, 3) + TILE, F32),
             pltpu.VMEM((4,) + slab, F32),
             pltpu.VMEM((1, 4, 4, 3) + TILE, F32),
             pltpu.VMEM((2, B, B), F32),
@@ -606,7 +647,7 @@
             pltpu.VMEM((2, 4, 4) + slab, F32),
             pltpu.VMEM((4, 2, 4, 3, B, B), F32),
             pltpu.VMEM((4, 2, 4, 3, B, B), F32),
-            DMA((3,)),
+            DMA((4,)),
             DMA((3, 4)),
             DMA((3,)),
             DMA((2, 2, 4, 4)),
@@ -617,6 +658,7 @@
             DMA((4, 2, 2, 4)),
         ]
         + gather_sems(4, 1)
+        + gather_sems(5, 1)
         + gather_sems(5, 4),
         compiler_params=pltpu.CompilerParams(
             collective_id=0, has_side_effects=True, vmem_limit_bytes=58 << 20
@@ -625,7 +667,7 @@
     )(block_map, children.reshape((2, 12) + slab), parent.reshape((24,) + slab), inverses)
 
 
-def parent_kernel(a_ref, u_ref, w_ref, pp_ref, g_ref, out_ref, panel, lth, ltl, q_ref, qcat, gcat, wh, wl):
+def parent_kernel(a_ref, u_ref, w_ref, pp_ref, g_ref, out_ref, panel, lth, ltl, q_ref, qcat, gcat, wh, wl, pairs, own, load_sem):
     f, y, x, z = place()
     steps = range(5)
     col = 4 * x + z
@@ -633,13 +675,21 @@
 
     @pl.when(n == 0)
     def _():
+        loads = [
+            pltpu.make_async_copy(pp_ref, pairs, load_sem.at[0]),
+            pltpu.make_async_copy(u_ref, own, load_sem.at[1]),
+        ]
+        for cp in loads:
+            cp.start()
+        for cp in loads:
+            cp.wait()
         for k in steps:
             for j in range(k):
-                block = pp_ref[PAIR[k, j]].reshape(B, B)
+                block = pairs[PAIR[k, j]].reshape(B, B)
                 panel[k * B : (k + 1) * B, j * B : (j + 1) * B] = block
                 panel[j * B : (j + 1) * B, k * B : (k + 1) * B] = block.T
             panel[k * B : (k + 1) * B, k * B : (k + 1) * B] = jnp.zeros((B, B), F32)
-            panel[k * B : (k + 1) * B, 5 * B :] = u_ref[k]
+            panel[k * B : (k + 1) * B, 5 * B :] = own[k]
             gcat[k] = rhs3(g_ref[k])
         for j in range(4):
             here, later = slice(j * B, (j + 1) * B), slice((j + 1) * B, 5 * B)
@@ -716,9 +766,9 @@
         grid=(6,),
         in_specs=[
             pl.BlockSpec((4, B, 3 * B), lambda n: (n, 0, 0)),
-            whole((5, B, 3 * B)),
+            ANY,
             pl.BlockSpec((1, 5, 4, 1) + TILE, lambda n: (n % 2, 0, 0, n // 2, 0, 0, 0, 0)),
-            whole((10,) + TILE),
+            ANY,
             whole((5, B, B)),
         ],
         out_specs=pl.BlockSpec((4, B, 3 * B), lambda n: (n, 0, 0)),
@@ -731,8 +781,11 @@
             pltpu.VMEM((5, 3 * B, B), BF16),
             pltpu.VMEM((4 * B, 5 * B), BF16),
             pltpu.VMEM((4 * B, 5 * B), BF16),
+            pltpu.VMEM((10,) + TILE, F32),
+            pltpu.VMEM((5, B, 3 * B), F32),
+            DMA((2,)),
         ],
-        compiler_params=pltpu.CompilerParams(vmem_limit_bytes=48 << 20),
+        compiler_params=pltpu.CompilerParams(vmem_limit_bytes=62 << 20),
         name="parent_update",
     )(a, u, w, pp, inverses)
 

time: 220 us -> 215 us (0.977)
  the two profiles are of different devices: /device:TPU:31 before, /device:TPU:1 now
where the time goes in v4:
time: 215 us; the launch traced here: 212 us
  Pallas kernels  211 us (98%)
    pallas_call x1, Pallas kernels, assemble(): pl.pallas_call(assemble_kernel, out_shape=(jax.ShapeDtypeStruct((24,) + s...  188 us
    pallas_call x1, Pallas kernels, parent_update(): pl.pallas_call(parent_kernel, out_shape=jax.ShapeDtypeStruct((24, B, 3 *...  23.6 us

profile of v4, /device:TPU:1, one launch (start us, length us, event | category | flops | bytes accessed | tf_op | source)
XLA Modules:
  0.0 211.6 jit_solution(1455474230428968964)
XLA Ops:
  0.0 187.8 %assemble.1 = (f32[24,128,384]{2,1,0:T(8,128)}, f32[5,128,384]{2,1,0:T(8,128)}, f32[2,5,4,3,4,2,16,128]{7,6,5,4,3,2,1,0:T(8,128)}, f32[10,4,2,16,128]{4,3,2,1,0:T(8,128)}) custom-call(s32[2,48]{1,0:T(2,128)} %map_ref.1, f32[2,12,128,384]{3,2,1,0:T(8,128)} %bitcast.3, f32[24,128,384]{2,1,0:T(8,128)} %bitcast.4, f32[2,2,128,128]{3,2,1,0:T(8,128)} %ginv_ref.1), custom_call_target="tpu_custom_call" | custom-call | tf_op jit(solution)/shard_map/assemble/pallas_call | solution.py:626
  187.8 23.6 %parent_update.1 = f32[24,128,384]{2,1,0:T(8,128)} custom-call(f32[24,128,384]{2,1,0:T(8,128)} %get-tuple-element.9.a_ref, f32[5,128,384]{2,1,0:T(8,128)} %get-tuple-element.10.u_ref, f32[2,5,4,3,4,2,16,128]{7,6,5,4,3,2,1,0:T(8,128)} %get-tuple-element.11.w_ref, f32[10,4,2,16,128]{4,3,2,1,0:T(8,128)} %get-tuple-element.12.pp_ref, f32[5,128,128]{2,1,0:T(8,128)} %g_ref.1), custom_call_target="tpu_custom_call" | custom-call | tf_op jit(solution)/shard_map/parent_update/pallas_call | solution.py:763
